TPU v7x, 512 devices: a whole 4x4x16 slice. The times are simulated.
512 devices in a mesh: node: 128 (over y, z, core), head: 4 (over x).
Axes of the slice: x: 4, y: 4, z: 16, core: 2. Of those that a mesh axis runs over, the one named last changes fastest.
Arguments:
- queries: bfloat16 [4096, 8192], P(('node', 'head')), may hold values from -128 to 128
- kv_cache: bfloat16 [2, 128, 512, 512], P(None, 'node', None, 'head'), may hold values from -6 to 6
- node_len: int32 [128], P('node'), may hold values from 128 to 512
- paths: int32 [4096, 4], P('node'), may hold values from 0 to 127, as said below
Outputs:
- attended: bfloat16 [4096, 8192], P(('node', 'head'))
Inputs may be any that keep to these rules, and one draw needn't show every extreme that they name: The rows' paths follow one tree of 128 nodes: 16 first-level nodes with one child each, each such child with two children, each of these with two leaf children; a row's entries are a first-level node and its descendants down to a leaf. In every aligned block of 32 rows (the rows of one index of node) each first-level node and its child lie on the paths of exactly 2 rows, and no node lies on more than 2 rows of the block.
All inputs are finite; a program needn't handle non-finite values.
Results may differ from a plain program's by a relative error of at most 0.0056.
Values may be sent and summed in bfloat16 or wider, within the bound.
A program may use at most 64 MiB of HBM per device.

v0:
```python
import jax
import jax.numpy as jnp
from jax import lax
from jax.sharding import PartitionSpec as P


def assign_slots(targets, n_dest, capacity):
    entry_count = targets.shape[0]
    onehot = (targets[:, None] == jnp.arange(n_dest, dtype=jnp.int32)[None, :]).astype(jnp.int32)
    before = jnp.cumsum(onehot, axis=0) - onehot
    slot_rank = jnp.sum(before * onehot, axis=1)
    slot_ids = targets * capacity + slot_rank
    slot_entry = (
        jnp.full((n_dest * capacity,), entry_count, jnp.int32)
        .at[slot_ids]
        .set(jnp.arange(entry_count, dtype=jnp.int32))
    )
    return (slot_ids, slot_entry)


def fill_slots(source, slot_entry, level_count):
    entry_count = source.shape[0] * level_count
    in_use = slot_entry < entry_count
    picked = source[jnp.where(in_use, slot_entry // level_count, 0)]
    return jnp.where(in_use[:, None], picked, jnp.zeros_like(picked))


def node_partials(received, key_rows, value_rows, length):
    n_src, slot_count, row_width = received.shape
    head_dim = key_rows.shape[-1]
    head_count = row_width // head_dim
    block_src = 16
    blocks = received.reshape(n_src // block_src, block_src * slot_count * head_count, head_dim)
    in_range = jnp.arange(key_rows.shape[0], dtype=jnp.int32) < length
    score_scale = head_dim ** (-0.5)

    def attend_block(query_block):
        scores = (
            jnp.einsum("qd,ld->ql", query_block, key_rows, preferred_element_type=jnp.float32)
            * score_scale
        )
        scores = jnp.where(in_range[None, :], scores, -jnp.inf)
        peak_score = jnp.max(scores, axis=1)
        probabilities = jnp.exp(scores - peak_score[:, None])
        total_sum = jnp.sum(probabilities, axis=1)
        partial_value = jnp.dot(
            probabilities.astype(jnp.bfloat16), value_rows, preferred_element_type=jnp.float32
        )
        return (partial_value.astype(jnp.bfloat16), peak_score, total_sum)

    partial_value, peak_score, total_sum = lax.map(attend_block, blocks)
    return (
        partial_value.reshape(n_src, slot_count, row_width),
        peak_score.reshape(n_src, slot_count, head_count),
        total_sum.reshape(n_src, slot_count, head_count),
    )


def merge_parts(outs, peaks, totals):
    top_peak = jnp.max(peaks, axis=1, keepdims=True)
    weight = jnp.exp(peaks - top_peak)
    numerator = jnp.sum(weight[..., None] * outs.astype(jnp.float32), axis=1)
    denominator = jnp.sum(weight * totals, axis=1)
    return numerator / denominator[..., None]


def shards(queries, kv_cache, node_len, paths):
    n_node = lax.axis_size("node")
    n_head = lax.axis_size("head")
    rows_dev, width_all = queries.shape
    group_rows, level_count = paths.shape
    head_dim = kv_cache.shape[-1]
    row_width = width_all // n_head
    head_count = row_width // head_dim
    key_rows = kv_cache[0, 0]
    value_rows = kv_cache[1, 0]
    length = node_len[0]
    capacity = group_rows * 8 // n_node
    by_group = queries.reshape(rows_dev, n_head, row_width)
    gathered = lax.all_to_all(by_group, "head", split_axis=1, concat_axis=0, tiled=True).reshape(
        group_rows, row_width
    )
    slot_ids, slot_entry = assign_slots(paths.reshape(-1), n_node, capacity)
    outgoing = fill_slots(gathered, slot_entry, level_count).reshape(n_node, capacity, row_width)
    part_out, part_peak, part_total = node_partials(
        lax.all_to_all(outgoing, "node", split_axis=0, concat_axis=0, tiled=True),
        key_rows,
        value_rows,
        length,
    )
    back_out = lax.all_to_all(part_out, "node", split_axis=0, concat_axis=0, tiled=True)
    back_peak = lax.all_to_all(part_peak, "node", split_axis=0, concat_axis=0, tiled=True)
    back_total = lax.all_to_all(part_total, "node", split_axis=0, concat_axis=0, tiled=True)
    back_out, back_peak, back_total = (back_out, back_peak, back_total)
    entry_out = back_out.reshape(n_node * capacity, head_count, head_dim)[slot_ids]
    entry_peak = back_peak.reshape(n_node * capacity, head_count)[slot_ids]
    entry_total = back_total.reshape(n_node * capacity, head_count)[slot_ids]
    merged = merge_parts(
        entry_out.reshape(group_rows, level_count, head_count, head_dim),
        entry_peak.reshape(group_rows, level_count, head_count),
        entry_total.reshape(group_rows, level_count, head_count),
    )
    finished = merged.astype(jnp.bfloat16).reshape(group_rows, 1, row_width)
    returned = lax.all_to_all(finished, "head", split_axis=0, concat_axis=1, tiled=True)
    return returned.reshape(rows_dev, width_all)


def solution(mesh):
    return jax.shard_map(
        shards,
        mesh=mesh,
        in_specs=(
            P(("node", "head"), None),
            P(None, "node", None, "head"),
            P("node"),
            P("node", None),
        ),
        out_specs=P(("node", "head"), None),
        check_vma=False,
    )
```

profile of v0, /device:TPU:1, one launch (start us, length us, event | category | flops | bytes accessed | tf_op | source)
XLA Modules:
  0.0 229.0 jit_solution(6609237779043215206)
XLA Ops:
  0.0 5.0 %all-to-all-start = ((bf16[8,4,2048]{2,0,1:T(8,128)(2,1)}), bf16[8,4,2048]{2,0,1:T(8,128)(2,1)S(1)}, u32[]{:S(2)}, u32[]{:S(2)}) async-start(bf16[8,4,2048]{2,0,1:T(8,128)(2,1)} %bitcast.60), calls=%async_computation | async-start | bytes 262144 | tf_op jit(solution)/shard_map/all_to_all | solution.py:80
  5.3 0.2 reduce_window_sum.11
  5.4 0.2 select_reduce_fusion
  5.8 1.0 scatter_custom_fusion
  6.9 0.2 broadcast_in_dim.56
  7.0 2.8 %all-to-all-done = bf16[8,4,2048]{2,0,1:T(8,128)(2,1)S(1)} async-done(((bf16[8,4,2048]{2,0,1:T(8,128)(2,1)}), bf16[8,4,2048]{2,0,1:T(8,128)(2,1)S(1)}, u32[]{:S(2)}, u32[]{:S(2)}) %all-to-all-start) | async-done | bytes 131104 | tf_op jit(solution)/shard_map/all_to_all | solution.py:80
  9.8 1.4 gather_fusion
  11.2 0.7 gather.15
  11.9 2.0 broadcast_select_fusion
  13.9 21.3 %all-to-all-start.1 = ((bf16[128,2,2048]{2,1,0:T(2,128)(2,1)}), bf16[128,2,2048]{2,1,0:T(2,128)(2,1)S(1)}, u32[]{:S(2)}, u32[]{:S(2)}) async-start(bf16[128,2,2048]{2,1,0:T(2,128)(2,1)} %broadcast_select_fusion), calls=%async_computation.1 | async-start | bytes 2097152 | tf_op jit(solution)/shard_map/all_to_all | solution.py:86
  35.3 54.3 %all-to-all-done.1 = bf16[128,2,2048]{2,1,0:T(2,128)(2,1)S(1)} async-done(((bf16[128,2,2048]{2,1,0:T(2,128)(2,1)}), bf16[128,2,2048]{2,1,0:T(2,128)(2,1)S(1)}, u32[]{:S(2)}, u32[]{:S(2)}) %all-to-all-start.1) | async-done | bytes 1048608 | tf_op jit(solution)/shard_map/all_to_all | solution.py:86
  89.6 0.7 reshape.116
  90.3 13.9 %while.15 = (s32[]{:T(128)}, bf16[8,512,128]{2,1,0:T(8,128)(2,1)S(1)}, f32[8,512]{1,0:T(8,128)S(1)}, f32[8,512]{1,0:T(8,128)S(1)}, bf16[8,512,128]{2,1,0:T(8,128...) while((s32[]{:T(128)}, ...), condition=%wide.region_6.7_spmd.clone, body=%wide.region_3.6_spmd.clone.sunk | while | flops 136117760 | bytes 3687545 | solution.py:51
  90.3 0.7 iota_compare_fusion.3
  90.9 0.3 fusion.31
  91.3 0.4 fusion.32
  91.7 0.2 fusion.33
  92.0 0.7 iota_compare_fusion.3
  92.7 0.3 fusion.31
  93.0 0.4 fusion.32
  93.4 0.2 fusion.33
  93.8 0.7 iota_compare_fusion.3
  94.4 0.3 fusion.31
  94.7 0.4 fusion.32
  95.2 0.2 fusion.33
  95.5 0.7 iota_compare_fusion.3
  96.2 0.3 fusion.31
  96.5 0.4 fusion.32
  96.9 0.2 fusion.33
  97.2 0.7 iota_compare_fusion.3
  97.9 0.3 fusion.31
  98.2 0.4 fusion.32
  98.6 0.2 fusion.33
  99.0 0.7 iota_compare_fusion.3
  99.6 0.3 fusion.31
  100.0 0.4 fusion.32
  100.4 0.2 fusion.33
  100.7 0.7 iota_compare_fusion.3
  101.4 0.3 fusion.31
  101.7 0.4 fusion.32
  102.1 0.2 fusion.33
  102.5 0.7 iota_compare_fusion.3
  103.1 0.3 fusion.31
  103.5 0.4 fusion.32
  103.9 0.2 fusion.33
  104.2 0.9 reshape.117
  105.1 8.5 %all-to-all-start.2 = ((f32[128,2,16]{2,1,0:T(2,128)}), f32[128,2,16]{2,1,0:T(2,128)S(1)}, u32[]{:S(2)}, u32[]{:S(2)}) async-start(f32[128,2,16]{2,1,0:T(2,128)} %reshape.117), calls=%async_computation.2 | async-start | bytes 262144 | tf_op jit(solution)/shard_map/all_to_all | solution.py:92
  113.5 0.9 reshape.122
  114.4 16.6 %all-to-all-done.2 = f32[128,2,16]{2,1,0:T(2,128)S(1)} async-done(((f32[128,2,16]{2,1,0:T(2,128)}), f32[128,2,16]{2,1,0:T(2,128)S(1)}, u32[]{:S(2)}, u32[]{:S(2)}) %all-to-all-start.2) | async-done | bytes 16416 | tf_op jit(solution)/shard_map/all_to_all | solution.py:92
  131.0 6.9 %all-to-all-start.4 = ((f32[128,2,16]{2,1,0:T(2,128)}), f32[128,2,16]{2,1,0:T(2,128)S(1)}, u32[]{:S(2)}, u32[]{:S(2)}) async-start(f32[128,2,16]{2,1,0:T(2,128)} %reshape.122), calls=%async_computation.4 | async-start | bytes 262144 | tf_op jit(solution)/shard_map/all_to_all | solution.py:93
  137.9 1.1 reshape.120
  139.0 16.4 %all-to-all-done.4 = f32[128,2,16]{2,1,0:T(2,128)S(1)} async-done(((f32[128,2,16]{2,1,0:T(2,128)}), f32[128,2,16]{2,1,0:T(2,128)S(1)}, u32[]{:S(2)}, u32[]{:S(2)}) %all-to-all-start.4) | async-done | bytes 16416 | tf_op jit(solution)/shard_map/all_to_all | solution.py:93
  155.4 7.1 %all-to-all-start.3 = ((bf16[128,2,2048]{2,1,0:T(2,128)(2,1)}), bf16[128,2,2048]{2,1,0:T(2,128)(2,1)S(1)}, u32[]{:S(2)}, u32[]{:S(2)}) async-start(bf16[128,2,2048]{2,1,0:T(2,128)(2,1)} %reshape.120), calls=%async_computation.3 | async-start | bytes 2097152 | tf_op jit(solution)/shard_map/all_to_all | solution.py:91
  162.5 0.6 gather_fusion.1
  163.2 0.6 gather_fusion.3
  163.9 53.1 %all-to-all-done.3 = bf16[128,2,2048]{2,1,0:T(2,128)(2,1)S(1)} async-done(((bf16[128,2,2048]{2,1,0:T(2,128)(2,1)}), bf16[128,2,2048]{2,1,0:T(2,128)(2,1)S(1)}, u32[]{:S(2)}, u32[]{:S(2)}) %all-to-all-start.3) | async-done | bytes 1048608 | tf_op jit(solution)/shard_map/all_to_all | solution.py:91
  217.0 0.7 reshape.121
  217.7 0.7 gather_fusion.2
  218.4 0.3 fusion.12
  218.9 0.5 broadcast.90
  219.4 1.4 reduce
  220.8 0.2 reshape.170
  221.0 7.2 %all_to_all.50 = bf16[4,2,8192]{2,1,0:T(2,128)(2,1)S(1)} all-to-all(bf16[4,2,8192]{2,1,0:T(2,128)(2,1)S(1)} %reshape.170), channel_id=1, replica_groups=mesh['node'=128,'head'=4] {'head'}, dimensions={0} | all-to-all | bytes 262144 | tf_op jit(solution)/shard_map/all_to_all | solution.py:104
  228.3 0.7 copy.14
  (40 shorter events, 1.9 us)
Async XLA Ops:
  0.0 5.0 %copy-start.1 = (s32[32,4]{0,1:T(4,128)S(1)}, s32[32,4]{0,1:T(4,128)}, u32[]{:S(2)}) copy-start(s32[32,4]{0,1:T(4,128)} %param.9) | copy-start | bytes 1540
  0.0 9.8 %all-to-all-start = ((bf16[8,4,2048]{2,0,1:T(8,128)(2,1)}), bf16[8,4,2048]{2,0,1:T(8,128)(2,1)S(1)}, u32[]{:S(2)}, u32[]{:S(2)}) async-start(bf16[8,4,2048]{2,0,1:T(8,128)(2,1)} %bitcast.60), calls=%async_computation | async-start | bytes 262144 | tf_op jit(solution)/shard_map/all_to_all | solution.py:80
  13.9 21.3 %copy-start = (bf16[2,1,512,128]{3,2,1,0:T(8,128)(2,1)S(1)}, bf16[2,1,512,128]{3,2,1,0:T(8,128)(2,1)}, u32[]{:S(2)}) copy-start(bf16[2,1,512,128]{3,2,1,0:T(8,128)(2,1)} %param.7) | copy-start | bytes 786436
  13.9 75.7 %all-to-all-start.1 = ((bf16[128,2,2048]{2,1,0:T(2,128)(2,1)}), bf16[128,2,2048]{2,1,0:T(2,128)(2,1)S(1)}, u32[]{:S(2)}, u32[]{:S(2)}) async-start(bf16[128,2,2048]{2,1,0:T(2,128)(2,1)} %broadcast_select_fusion), calls=%async_computation.1 | async-start | bytes 2097152 | tf_op jit(solution)/shard_map/all_to_all | solution.py:86
  105.1 25.9 %all-to-all-start.2 = ((f32[128,2,16]{2,1,0:T(2,128)}), f32[128,2,16]{2,1,0:T(2,128)S(1)}, u32[]{:S(2)}, u32[]{:S(2)}) async-start(f32[128,2,16]{2,1,0:T(2,128)} %reshape.117), calls=%async_computation.2 | async-start | bytes 262144 | tf_op jit(solution)/shard_map/all_to_all | solution.py:92
  131.0 24.4 %all-to-all-start.4 = ((f32[128,2,16]{2,1,0:T(2,128)}), f32[128,2,16]{2,1,0:T(2,128)S(1)}, u32[]{:S(2)}, u32[]{:S(2)}) async-start(f32[128,2,16]{2,1,0:T(2,128)} %reshape.122), calls=%async_computation.4 | async-start | bytes 262144 | tf_op jit(solution)/shard_map/all_to_all | solution.py:93
  155.4 61.6 %all-to-all-start.3 = ((bf16[128,2,2048]{2,1,0:T(2,128)(2,1)}), bf16[128,2,2048]{2,1,0:T(2,128)(2,1)S(1)}, u32[]{:S(2)}, u32[]{:S(2)}) async-start(bf16[128,2,2048]{2,1,0:T(2,128)(2,1)} %reshape.120), calls=%async_computation.3 | async-start | bytes 2097152 | tf_op jit(solution)/shard_map/all_to_all | solution.py:91
where the time goes:
time: 232 us; the launch traced here: 229 us
  waiting for transfers between devices  143 us (62%)
  starting transfers between devices  48.7 us (21%)
  local copies, waits for them, and re-layouts  12.4 us (5%)
  other arithmetic  11.2 us (5%)
  blocking collectives  7.21 us (3%)
  matrix products  5.89 us (3%)
    all_to_all x1, waiting for transfers between devices, shards(): lax.all_to_all(outgoing, 'node', split_axis=0, concat_axis=0, tiled=True)  54.3 us
    all_to_all x1, waiting for transfers between devices, shards(): lax.all_to_all(part_out, 'node', split_axis=0, concat_axis=0, tiled=True)  53.1 us
    all_to_all x1, starting transfers between devices, shards(): lax.all_to_all(outgoing, 'node', split_axis=0, concat_axis=0, tiled=True)  21.3 us
    all_to_all x1, waiting for transfers between devices, shards(): lax.all_to_all(part_peak, 'node', split_axis=0, concat_axis=0, tiled=True)  16.6 us
    all_to_all x1, waiting for transfers between devices, shards(): lax.all_to_all(part_total, 'node', split_axis=0, concat_axis=0, tiled=True)  16.4 us
    all_to_all x1, starting transfers between devices, shards(): lax.all_to_all(part_peak, 'node', split_axis=0, concat_axis=0, tiled=True)  8.48 us
    all_to_all x1, blocking collectives, shards(): lax.all_to_all(finished, 'head', split_axis=0, concat_axis=1, tiled=True)  7.21 us
    all_to_all x1, starting transfers between devices, shards(): lax.all_to_all(part_out, 'node', split_axis=0, concat_axis=0, tiled=True)  7.12 us
  transfers between devices with their start and end apart: 5, of which 5 were waited for; matrix products, arithmetic and copies ran while one was open for 2% of the time, Pallas kernels for 0%

commit v1 on v0

v1 whole, which is shorter than its diff:
```python
import functools
import math

import jax
import jax.numpy as jnp
from jax import lax
from jax.experimental import pallas as pl
from jax.experimental.pallas import tpu as pltpu
from jax.sharding import PartitionSpec as P

MESH = pl.DeviceIdType.MESH
NX, NY, NZ, NC = 4, 4, 16, 2
PLANE = NY * NC
FAR = NZ // 2
ROWS, GROUP, DIM, TOKENS, DEPTH = 32, 16, 128, 512, 4
PAIRS = ROWS // 2
HALF = ROWS // 2
OWN = ROWS // NX
EMPTY = -1e30
SCALE = math.log2(math.e) / math.sqrt(DIM)
FLOWS = ((0, 0), (1, 1), (0, 1), (1, 0))


def reach(side, half):
    return FAR if side == half else FAR - 1


def slot(side, hop):
    return hop % NZ if side == 0 else (NZ - hop) % NZ


def kernel(
    q_ref, kv_ref, meta_ref, meta_s, len_s, out_ref,
    qx, q0, qall, kvall, lens, bias, metav, metas, part_o, part_m, part_l,
    loc_o, loc_s, o_in, o_out, s_in, s_out, fin, fx,
    x_send, x_recv, kv_send, kv_recv, ln_send, ln_recv, q_send, q_recv, m_send, m_recv,
    ms_sem, o_send, o_recv, st_send, st_recv, r_send, r_recv, own_sem,
):
    node = lax.axis_index("node")
    x = lax.axis_index("head")
    core = lax.rem(node, NC)
    z = lax.rem(node // NC, NZ)
    y = node // (NC * NZ)

    def dev(yy, zz, cc, xx):
        return ((yy * NZ + zz) * NC + cc, xx)

    z_up, z_down = lax.rem(z + 1, NZ), lax.rem(z + NZ - 1, NZ)
    out_dev = (dev(y, z_up, core, x), dev(y, z_down, core, x))
    back_dev = (out_dev[1], out_dev[0])
    mate = dev(y, z, 1 - core, x)
    y_dev = [None] + [dev(lax.rem(y + d, NY), z, core, x) for d in range(1, NY)]
    x_dev = [None] + [dev(y, z, core, lax.rem(x + d, NX)) for d in range(1, NX)]

    barrier = pltpu.get_barrier_semaphore()
    partners = [out_dev[0], out_dev[1], mate] + y_dev[1:] + x_dev[1:]
    for partner in partners:
        pl.semaphore_signal(barrier, inc=1, device_id=partner, device_id_type=MESH)
    pl.semaphore_wait(barrier, len(partners))

    def remote(src, dst, send, recv, to):
        return pltpu.make_async_remote_copy(
            src_ref=src, dst_ref=dst, send_sem=send, recv_sem=recv, device_id=to, device_id_type=MESH)

    def x_copy(d):
        heads = pl.ds(pl.multiple_of(lax.rem(x + d, NX) * GROUP, GROUP), GROUP)
        rows = pl.ds(pl.multiple_of(x * OWN, OWN), OWN)
        if d == 0:
            return pltpu.make_async_copy(q_ref.at[:, heads, :], qx.at[rows], own_sem.at[0])
        return remote(q_ref.at[:, heads, :], qx.at[rows], x_send.at[d], x_recv.at[d], x_dev[d])

    for d in (1, 2, 3, 0):
        x_copy(d).start()

    def node_of(yy, cc):
        return yy * NC + cc

    own_k = node_of(y, core)
    lens[own_k] = jnp.full(lens.shape[1:], len_s[0], jnp.int32)
    kv_own = pltpu.make_async_copy(kv_ref.at[:, 0], kvall.at[own_k], own_sem.at[1])
    kv_own.start()

    def kv_copies(kind, d):
        if kind == 0:
            k = own_k
            to = mate if d == 0 else y_dev[d]
            src = kv_ref.at[:, 0]
        else:
            k = node_of(lax.rem(y + NY - d, NY), core)
            to = mate
            src = kvall.at[k]
        i = d if kind == 0 else NY + d
        return (
            remote(src, kvall.at[k], kv_send.at[i], kv_recv.at[i], to),
            remote(lens.at[k], lens.at[k], ln_send.at[i], ln_recv.at[i], to),
        )

    for d in (2, 1, 3, 0):
        for copy in kv_copies(0, d):
            copy.start()

    for d in (0, 1, 2, 3):
        if d == 0:
            x_copy(d).wait()
        else:
            x_copy(d).wait_recv()
    for p in range(ROWS):
        q0[p // 2, (p % 2) * GROUP:(p % 2 + 1) * GROUP, :] = qx[meta_s[2, p]]

    def q_copy(side, half, hop):
        part = pl.ds(half * (PAIRS // 2), PAIRS // 2)
        src = q0.at[part] if hop == 1 else qall.at[slot(side, hop - 1), part]
        return remote(src, qall.at[slot(side, hop), part], q_send.at[side, half, hop - 1],
                      q_recv.at[side, half, hop - 1], out_dev[side])

    def m_copy(side, hop):
        src = meta_ref if hop == 1 else metav.at[slot(side, hop - 1)]
        return remote(src, metav.at[slot(side, hop)], m_send.at[side, hop - 1],
                      m_recv.at[side, hop - 1], out_dev[side])

    def m_local(i):
        src = meta_ref if i == 0 else metav.at[i]
        return pltpu.make_async_copy(src, metas.at[i], ms_sem.at[i])

    for side, half in FLOWS:
        q_copy(side, half, 1).start()
    for side in (0, 1):
        m_copy(side, 1).start()
    m_local(0).start()

    part_o[...] = jnp.zeros_like(part_o)
    part_l[...] = jnp.zeros_like(part_l)
    part_m[...] = jnp.full_like(part_m, EMPTY)

    lane = lax.broadcasted_iota(jnp.int32, (GROUP, DIM), 1)

    def attend(blocks):
        for k in range(PLANE):
            n = ((k // NC) * NZ + z) * NC + k % NC
            tiles = [ref[metas[i, 0, n]] for ref, i in blocks]
            lhs = tiles[0] if len(tiles) == 1 else jnp.concatenate(tiles, axis=0)
            score = lax.dot_general(lhs, kvall[k, 0], (((1,), (1,)), ((), ())),
                                    preferred_element_type=jnp.float32)
            score = score + bias[k:k + 1, :]
            peak = jnp.max(score, axis=1, keepdims=True)
            prob = jnp.exp2((score - peak) * SCALE)
            total = jnp.sum(prob, axis=1, keepdims=True)
            value = jnp.dot(prob.astype(jnp.bfloat16), kvall[k, 1], preferred_element_type=jnp.float32)
            for b in range(len(blocks)):
                rows = slice(b * 2 * GROUP, (b + 1) * 2 * GROUP)
                part_o[b, k] = value[rows]
                part_m[b, k] = jnp.broadcast_to(peak[rows], (2 * GROUP, DIM))
                part_l[b, k] = jnp.broadcast_to(total[rows], (2 * GROUP, DIM))

    def merge_rows(b, i, half, keep):
        stat = jnp.zeros((GROUP, DIM), jnp.float32)
        for r in range(HALF):
            p = half * HALF + r
            sub = slice((p % 2) * GROUP, (p % 2 + 1) * GROUP)
            ks = []
            for j in range(DEPTH):
                t = metas[i, 1, p * DEPTH + j] - z * NZ
                ks.append(jnp.where((t >= 0) & (t < PLANE), t, PLANE))
            peaks = [part_m[b, k, sub, :] for k in ks]
            top = jnp.maximum(jnp.maximum(peaks[0], peaks[1]), jnp.maximum(peaks[2], peaks[3]))
            total = jnp.zeros((GROUP, DIM), jnp.float32)
            value = jnp.zeros((GROUP, DIM), jnp.float32)
            for k, peak in zip(ks, peaks):
                weight = jnp.exp2((peak - top) * SCALE)
                total = total + weight * part_l[b, k, sub, :]
                value = value + weight * part_o[b, k, sub, :]
            loc_o[keep, p] = value
            stat = jnp.where(lane == r, top, jnp.where(lane == r + HALF, total, stat))
        loc_s[keep, half] = stat

    def weights(a, c):
        top = jnp.maximum(a, c)
        wa, wc = jnp.exp2((a - top) * SCALE), jnp.exp2((c - top) * SCALE)
        total = pltpu.roll(wa, HALF, 1) * a + pltpu.roll(wc, HALF, 1) * c
        return wa, wc, jnp.where(lane < HALF, top, total)

    def column(tile, r):
        return jnp.broadcast_to(tile[:, r:r + 1], (GROUP, DIM))

    def o_copies(side, half, d):
        return (
            remote(o_out.at[side, half, d - 1], o_in.at[side, half, d - 1], o_send.at[side, half, d - 1],
                   o_recv.at[side, half, d - 1], back_dev[side]),
            remote(s_out.at[side, half, d - 1], s_in.at[side, half, d - 1], st_send.at[side, half, d - 1],
                   st_recv.at[side, half, d - 1], back_dev[side]),
        )

    def first_out(side, half, d, keep):
        for r in range(HALF):
            o_out[side, half, d - 1, r] = loc_o[keep, half * HALF + r].astype(jnp.bfloat16)
        s_out[side, half, d - 1] = loc_s[keep, half]
        for copy in o_copies(side, half, d):
            copy.start()

    def add_out(side, half, d, keep):
        for copy in o_copies(side, half, d + 1):
            copy.wait_recv()
        wa, wc, stat = weights(s_in[side, half, d], loc_s[keep, half])
        s_out[side, half, d - 1] = stat
        for r in range(HALF):
            total = (column(wa, r) * o_in[side, half, d, r].astype(jnp.float32)
                     + column(wc, r) * loc_o[keep, half * HALF + r])
            o_out[side, half, d - 1, r] = total.astype(jnp.bfloat16)
        for copy in o_copies(side, half, d):
            copy.start()

    for hop in range(1, FAR + 1):
        for side, half in FLOWS:
            if hop <= reach(side, half):
                q_copy(side, half, hop).wait_recv()
                if hop < reach(side, half):
                    q_copy(side, half, hop + 1).start()
        for side in (0, 1):
            if hop <= reach(side, 0):
                m_copy(side, hop).wait_recv()
                if hop < reach(side, 0):
                    m_copy(side, hop + 1).start()
                m_local(slot(side, hop)).start()
        if hop == 5:
            for d in (1, 3, 2):
                for copy, onward in zip(kv_copies(0, d), kv_copies(1, d)):
                    copy.wait_recv()
                    onward.start()
    kv_own.wait()
    for copy in kv_copies(0, 0):
        copy.wait_recv()
    for d in (1, 3, 2):
        for copy in kv_copies(1, d):
            copy.wait_recv()
    token = lax.broadcasted_iota(jnp.int32, (1, TOKENS), 1)
    for k in range(PLANE):
        length = jnp.concatenate([lens[k, 0:1, :]] * (TOKENS // DIM), axis=1)
        bias[k:k + 1, :] = jnp.where(token < length, 0.0, EMPTY)
    for i in range(NZ):
        m_local(i).wait()

    attend([(qall.at[FAR], FAR)])
    for half in (0, 1):
        merge_rows(0, FAR, half, 0)
        first_out(half, half, FAR, 0)

    def near(d, first):
        attend([(qall.at[d], d), (qall.at[NZ - d], NZ - d)])
        for side, half in FLOWS:
            merge_rows(side, (d, NZ - d)[side], half, side)
            if first and side != half:
                first_out(side, half, d, side)
            else:
                add_out(side, half, d, side)

    near(FAR - 1, True)

    def step(t, carry):
        near(FAR - 2 - t, False)
        return carry

    lax.fori_loop(0, FAR - 2, step, 0)

    attend([(q0, 0)])
    for half in (0, 1):
        merge_rows(0, 0, half, 0)
        for side in (0, 1):
            for copy in o_copies(side, half, 1):
                copy.wait_recv()
        a, c, own = s_in[0, half, 0], s_in[1, half, 0], loc_s[0, half]
        top = jnp.maximum(jnp.maximum(a, c), own)
        wa, wc, wo = (jnp.exp2((v - top) * SCALE) for v in (a, c, own))
        total = (pltpu.roll(wa, HALF, 1) * a + pltpu.roll(wc, HALF, 1) * c + pltpu.roll(wo, HALF, 1) * own)
        share = 1.0 / jnp.where(lane >= HALF, jnp.where(lane < 2 * HALF, total, 1.0), 1.0)
        share = pltpu.roll(share, DIM - HALF, 1)
        wa, wc, wo = wa * share, wc * share, wo * share
        for r in range(HALF):
            p = half * HALF + r
            value = (column(wa, r) * o_in[0, half, 0, r].astype(jnp.float32)
                     + column(wc, r) * o_in[1, half, 0, r].astype(jnp.float32)
                     + column(wo, r) * loc_o[0, p])
            fin[p] = value.astype(jnp.bfloat16)

    for r in range(ROWS):
        fx[r] = fin[meta_s[2, ROWS + r]]

    def r_copy(d):
        rows = pl.ds(pl.multiple_of(lax.rem(x + d, NX) * OWN, OWN), OWN)
        heads = pl.ds(pl.multiple_of(x * GROUP, GROUP), GROUP)
        if d == 0:
            return pltpu.make_async_copy(fx.at[rows], out_ref.at[:, heads, :], own_sem.at[2])
        return remote(fx.at[rows], out_ref.at[:, heads, :], r_send.at[d], r_recv.at[d], x_dev[d])

    for d in (1, 2, 3, 0):
        r_copy(d).start()
    for d in (1, 2, 3):
        x_copy(d).wait_send()
    for d in range(NY):
        for kind in (0, 1):
            if kind == 0 or d > 0:
                for copy in kv_copies(kind, d):
                    copy.wait_send()
    for hop in range(1, FAR + 1):
        for side, half in FLOWS:
            if hop <= reach(side, half):
                q_copy(side, half, hop).wait_send()
                for copy in o_copies(side, half, hop):
                    copy.wait_send()
        for side in (0, 1):
            if hop <= reach(side, 0):
                m_copy(side, hop).wait_send()
    r_copy(0).wait()
    for d in (1, 2, 3):
        r_copy(d).wait()


def plan(paths):
    row = jnp.arange(ROWS, dtype=jnp.int32)
    key = paths[:, 0] * ROWS + row
    place = jnp.sum((key[None, :] < key[:, None]).astype(jnp.int32), axis=1)
    at = (place[None, :] == row[:, None]).astype(jnp.int32)
    order = jnp.sum(at * row[None, :], axis=1)
    ordered = jnp.sum(at[:, :, None] * paths[None, :, :], axis=1)
    nodes = jnp.arange(PLANE * NZ, dtype=jnp.int32)
    pair = jnp.max(jnp.where(ordered[:, :, None] == nodes, (row // 2)[:, None, None], 0), axis=(0, 1))
    visit = (lax.rem(ordered // NC, NZ) * NZ + ordered // (NC * NZ) * NC + lax.rem(ordered, NC)).reshape(-1)
    spare = jnp.zeros((DIM - 2 * ROWS,), jnp.int32)
    table = jnp.stack([pair, visit, jnp.concatenate([order, place, spare])])
    return jnp.concatenate([table, jnp.zeros((5, DIM), jnp.int32)], axis=0)


def shards(queries, kv_cache, node_len, paths):
    rows, width = queries.shape
    meta = plan(paths)
    bf16, f32, i32 = jnp.bfloat16, jnp.float32, jnp.int32
    dma = pltpu.SemaphoreType.DMA
    vmem, smem = pl.BlockSpec(memory_space=pltpu.VMEM), pl.BlockSpec(memory_space=pltpu.SMEM)
    out = pl.pallas_call(
        kernel,
        out_shape=jax.ShapeDtypeStruct((OWN, NX * GROUP, DIM), bf16),
        in_specs=[vmem, pl.BlockSpec(memory_space=pl.ANY), vmem, smem, smem],
        out_specs=vmem,
        scratch_shapes=[
            pltpu.VMEM((ROWS, GROUP, DIM), bf16),
            pltpu.VMEM((PAIRS, 2 * GROUP, DIM), bf16),
            pltpu.VMEM((NZ, PAIRS, 2 * GROUP, DIM), bf16),
            pltpu.VMEM((PLANE, 2, TOKENS, DIM), bf16),
            pltpu.VMEM((PLANE, 8, DIM), i32),
            pltpu.VMEM((PLANE, TOKENS), f32),
            pltpu.VMEM((NZ, 8, DIM), i32),
            pltpu.SMEM((NZ, 8, DIM), i32),
            pltpu.VMEM((2, PLANE + 1, 2 * GROUP, DIM), f32),
            pltpu.VMEM((2, PLANE + 1, 2 * GROUP, DIM), f32),
            pltpu.VMEM((2, PLANE + 1, 2 * GROUP, DIM), f32),
            pltpu.VMEM((2, ROWS, GROUP, DIM), f32),
            pltpu.VMEM((2, 2, GROUP, DIM), f32),
            pltpu.VMEM((2, 2, FAR, HALF, GROUP, DIM), bf16),
            pltpu.VMEM((2, 2, FAR, HALF, GROUP, DIM), bf16),
            pltpu.VMEM((2, 2, FAR, GROUP, DIM), f32),
            pltpu.VMEM((2, 2, FAR, GROUP, DIM), f32),
            pltpu.VMEM((ROWS, GROUP, DIM), bf16),
            pltpu.VMEM((ROWS, GROUP, DIM), bf16),
            dma((NX,)), dma((NX,)),
            dma((2 * NY,)), dma((2 * NY,)),
            dma((2 * NY,)), dma((2 * NY,)),
            dma((2, 2, FAR)), dma((2, 2, FAR)),
            dma((2, FAR)), dma((2, FAR)),
            dma((NZ,)),
            dma((2, 2, FAR)), dma((2, 2, FAR)),
            dma((2, 2, FAR)), dma((2, 2, FAR)),
            dma((NX,)), dma((NX,)),
            dma((3,)),
        ],
        compiler_params=pltpu.CompilerParams(
            collective_id=0, has_side_effects=True, vmem_limit_bytes=40 * 1024 * 1024),
        cost_estimate=pl.CostEstimate(flops=1 << 30, bytes_accessed=1 << 22, transcendentals=1 << 21),
    )(queries.reshape(rows, NX * GROUP, DIM), kv_cache, meta, meta, node_len)
    return out.reshape(rows, width)


def solution(mesh):
    return jax.shard_map(
        shards,
        mesh=mesh,
        in_specs=(
            P(("node", "head"), None),
            P(None, "node", None, "head"),
            P("node"),
            P("node", None),
        ),
        out_specs=P(("node", "head"), None),
        check_vma=False,
    )
```

time: 232 us -> 97.4 us (0.42)
  the two profiles are of different devices: /device:TPU:1 before, /device:TPU:4 now
where the time goes in v1:
time: 97.4 us; the launch traced here: 97.2 us
  Pallas kernels  93.8 us (96%)
  local copies, waits for them, and re-layouts  1.95 us (2%)
    pallas_call x1, Pallas kernels, shards(): pl.pallas_call(kernel, out_shape=jax.ShapeDtypeStruct((OWN, NX * GROUP, D...  93.8 us

profile of v1, /device:TPU:4, one launch (start us, length us, event | category | flops | bytes accessed | tf_op | source)
XLA Modules:
  0.0 97.2 jit_solution(13054099720574952311)
XLA Ops:
  0.0 0.0 copy-start.1
  0.0 0.0 copy-start
  0.7 0.0 copy-done.1
  0.7 0.2 convert_reduce_fusion
  0.9 0.1 select_reduce_fusion.1
  1.0 0.1 pad.3.clone
  1.1 0.1 add_bitcast_fusion
  1.2 0.1 multiply_reduce_fusion
  1.4 0.1 select_reduce_fusion
  1.5 0.1 copy.7
  1.6 0.1 reduce_sum.31
  1.7 0.1 add_add_fusion.meta_ref.meta_s
  1.8 0.9 copy.13
  2.7 0.0 copy-done
  2.7 93.8 %shard_map.46 = bf16[8,64,128]{2,1,0:T(8,128)(2,1)S(1)} custom-call(bf16[8,64,128]{2,1,0:T(8,128)(2,1)S(1)} %bitcast.16, bf16[2,1,512,128]{3,2,1,0:T(8,128)(2,1)S(1)} %copy-done, s32[8,128]{1,0:T(8,128)S(1)} %add_add_fusion.meta_ref.meta_s, s32[8,128]{1,0:T(8,128)S(1)} %add_add_fusion.meta_ref.meta_s, s32[1]{0:T(128)S(6)} %copy.14.len_s), custom_call_target="tpu_custom_call" | custom-call | flops 1073741824 | bytes 4194304 | tf_op jit(solution)/shard_map/pallas_call | solution.py:338
  96.5 0.7 copy.12
  (7 shorter events, 0.0 us)
Async XLA Ops:
  0.0 0.7 copy-start.1
  0.0 2.7 %copy-start = (bf16[2,1,512,128]{3,2,1,0:T(8,128)(2,1)S(1)}, bf16[2,1,512,128]{3,2,1,0:T(8,128)(2,1)}, u32[]{:S(2)}) copy-start(bf16[2,1,512,128]{3,2,1,0:T(8,128)(2,1)} %kv_ref.1) | copy-start | bytes 786436

commit v2 on v0

v2 whole, which is shorter than its diff:
```python
import math

import jax
import jax.numpy as jnp
from jax import lax
from jax.experimental import pallas as pl
from jax.experimental.pallas import tpu as pltpu
from jax.sharding import PartitionSpec as P

MESH = pl.DeviceIdType.MESH
NX, NY, NZ, NC = 4, 4, 16, 2
PLANE = NY * NC
FAR = NZ // 2
ROWS, GROUP, DIM, TOKENS, DEPTH = 32, 16, 128, 512, 4
PAIRS = ROWS // 2
PAIR = 2 * GROUP
OWN = ROWS // NX
SUB = 8
EMPTY = -1e30
SCALE = math.log2(math.e) / math.sqrt(DIM)
WARM = 6
PER = 2 * (FAR + 1)


def ring_slot(side, hop):
    return hop if side == 0 else lax.rem(NZ - hop, NZ)


def kernel(
    q_ref, kv_ref, meta_ref, meta_s, len_s, out_ref,
    qx, qplane, kvz, lens, metav, metas, o_out, o_in, s_out, s_in, fin, fx,
    x_send, x_recv, kv_send, kv_recv, ln_send, ln_recv, q_send, q_recv, m_send, m_recv,
    ms_sem, o_send, o_recv, s_send, s_recv, r_send, r_recv, own_sem,
):
    node = lax.axis_index("node")
    x = lax.axis_index("head")
    core = lax.rem(node, NC)
    z = lax.rem(node // NC, NZ)
    y = node // (NC * NZ)

    def dev(yy, zz, cc, xx):
        return ((yy * NZ + zz) * NC + cc, xx)

    z_dev = (dev(y, lax.rem(z + 1, NZ), core, x), dev(y, lax.rem(z + NZ - 1, NZ), core, x))
    x_dev = [None] + [dev(y, z, core, lax.rem(x + d, NX)) for d in range(1, NX)]
    p_dev = [dev(lax.rem(y + j // NC, NY), z, lax.rem(core + j % NC, NC), x) for j in range(PLANE)]
    b_dev = [dev(lax.rem(y + NY - j // NC, NY), z, lax.rem(core + j % NC, NC), x) for j in range(PLANE)]

    barrier = pltpu.get_barrier_semaphore()
    partners = list(z_dev) + x_dev[1:] + p_dev[1:]
    for partner in partners:
        pl.semaphore_signal(barrier, inc=1, device_id=partner, device_id_type=MESH)
    pl.semaphore_wait(barrier, len(partners))

    def remote(src, dst, send, recv, to):
        return pltpu.make_async_remote_copy(
            src_ref=src, dst_ref=dst, send_sem=send, recv_sem=recv, device_id=to, device_id_type=MESH)

    def x_copy(d):
        heads = pl.ds(pl.multiple_of(lax.rem(x + d, NX) * GROUP, GROUP), GROUP)
        rows = pl.ds(pl.multiple_of(x * OWN, OWN), OWN)
        if d == 0:
            return pltpu.make_async_copy(q_ref.at[:, heads, :], qx.at[rows], own_sem.at[0])
        return remote(q_ref.at[:, heads, :], qx.at[rows], x_send.at[d], x_recv.at[d], x_dev[d])

    for d in (2, 1, 3, 0):
        x_copy(d).start()

    def first_kv(side, part):
        return remote(kv_ref.at[part, 0], kvz.at[ring_slot(side, 1), part], kv_send.at[side, part, 0],
                      kv_recv.at[side, part, 0], z_dev[side])

    def kv_copy(side, part, hop):
        return remote(kvz.at[ring_slot(side, hop - 1), part], kvz.at[ring_slot(side, hop), part],
                      kv_send.at[side, part, hop - 1], kv_recv.at[side, part, hop - 1], z_dev[side])

    def ln_copy(side, hop):
        return remote(lens.at[ring_slot(side, hop - 1)], lens.at[ring_slot(side, hop)],
                      ln_send.at[side, hop - 1], ln_recv.at[side, hop - 1], z_dev[side])

    lens[0] = jnp.full(lens.shape[1:], len_s[0], jnp.int32)
    for part in (0, 1):
        for side in (0, 1):
            first_kv(side, part).start()
        if part == 0:
            for side in (0, 1):
                ln_copy(side, 1).start()
    kv_own = [pltpu.make_async_copy(kv_ref.at[part, 0], kvz.at[0, part], own_sem.at[1 + part]) for part in (0, 1)]
    for copy in kv_own:
        copy.start()

    x_copy(0).wait()
    for d in (1, 3, 2):
        x_copy(d).wait_recv()
    for p in range(ROWS):
        qplane[0, p // 2, (p % 2) * GROUP:(p % 2 + 1) * GROUP, :] = qx[meta_s[2, p]]

    def q_copies(j):
        return (
            remote(qplane.at[0], qplane.at[j], q_send.at[j], q_recv.at[j], p_dev[j]),
            remote(meta_ref, metav.at[j], m_send.at[j], m_recv.at[j], p_dev[j]),
        )

    for j in (4, 5, 2, 3, 6, 7, 1):
        for copy in q_copies(j):
            copy.start()

    def m_local(j):
        src = meta_ref if j == 0 else metav.at[j]
        return pltpu.make_async_copy(src, metas.at[j], ms_sem.at[j])

    m_local(0).start()

    def relay(hop, part):
        for side in (0, 1):
            reach = FAR - 1 + (part + side + 1) % 2

            @pl.when(hop <= reach)
            def _(side=side):
                kv_copy(side, part, hop).wait_recv()

            @pl.when(hop < reach)
            def _(side=side):
                kv_copy(side, part, hop + 1).start()

            @pl.when((part == 0) & (hop <= FAR - side))
            def _(side=side):
                ln_copy(side, hop).wait_recv()

            @pl.when((part == 0) & (hop < FAR - side))
            def _(side=side):
                ln_copy(side, hop + 1).start()

    lane = lax.broadcasted_iota(jnp.int32, (SUB, DIM), 1)
    token = lax.broadcasted_iota(jnp.int32, (1, TOKENS), 1)

    def attend(i, hop, side):
        n = (y * NZ + lax.rem(z + NZ - i, NZ)) * NC + core
        length = jnp.concatenate([lens[i, 0:1, :]] * (TOKENS // DIM), axis=1)
        bias = jnp.where(token < length, 0.0, EMPTY)
        for j0 in range(0, PLANE, 4):
            lhs = jnp.concatenate([qplane[j, metas[j, 0, n]] for j in range(j0, j0 + 4)], axis=0)
            score = lax.dot_general(lhs, kvz[i, 0], (((1,), (1,)), ((), ())),
                                    preferred_element_type=jnp.float32) + bias
            peak = jnp.max(score, axis=1, keepdims=True)
            prob = jnp.exp2((score - peak) * SCALE)
            total = jnp.sum(prob, axis=1, keepdims=True)
            value = jnp.dot(prob.astype(jnp.bfloat16), kvz[i, 1],
                            preferred_element_type=jnp.float32).astype(jnp.bfloat16)
            for j in range(j0, j0 + 4):
                base = (j - j0) * PAIR
                at = j * PER + 2 * hop + side
                stat = jnp.zeros((SUB, DIM), jnp.float32)
                for c in range(PAIR // SUB):
                    rows = slice(base + c * SUB, base + (c + 1) * SUB)
                    stat = jnp.where(lane == c, peak[rows], stat)
                    stat = jnp.where(lane == c + PAIR // SUB, total[rows], stat)
                (o_in if j == 0 else o_out)[at] = value[base:base + PAIR]
                (s_in if j == 0 else s_out)[at] = stat

    def back_copies(j, hop, count):
        at = pl.ds(j * PER + 2 * hop, count)
        return (
            remote(o_out.at[at], o_in.at[at], o_send.at[j, hop], o_recv.at[j, hop], b_dev[j]),
            remote(s_out.at[at], s_in.at[at], s_send.at[j, hop], s_recv.at[j, hop], b_dev[j]),
        )

    for u in range(WARM):
        relay(u // 2 + 1, u % 2)
    for j in range(1, PLANE):
        for copy in q_copies(j):
            copy.wait_recv()
        m_local(j).start()
    for copy in kv_own:
        copy.wait()
    for j in range(PLANE):
        m_local(j).wait()

    def half_hop(u, carry):
        relay(u // 2 + 1, lax.rem(u, 2))
        hop = u - WARM
        attend(hop, hop, 0)
        attend(lax.rem(NZ - hop, NZ), hop, 1)
        for j in range(1, PLANE):
            for copy in back_copies(j, hop, 2):
                copy.start()
        return carry

    lax.fori_loop(WARM, WARM + FAR, half_hop, 0)
    for u in range(WARM + FAR, 2 * FAR):
        relay(u // 2 + 1, u % 2)
    attend(FAR, FAR, 0)
    for j in (4, 5, 2, 3, 6, 7, 1):
        for copy in back_copies(j, FAR, 1):
            copy.start()

    for hop in range(FAR + 1):
        for j in range(1, PLANE):
            for copy in back_copies(j, hop, 2 if hop < FAR else 1):
                copy.wait_recv()

    def column(tile, c):
        return jnp.concatenate(
            [jnp.broadcast_to(tile[:, c + h:c + h + 1], (SUB, DIM)) for h in range(GROUP // SUB)], axis=0)

    for p in range(ROWS):
        s = p % 2
        at = [meta_s[1, p * DEPTH + j] for j in range(DEPTH)]
        stats = [s_in[a] for a in at]
        peaks = [column(t, 2 * s) for t in stats]
        totals = [column(t, 2 * s + PAIR // SUB) for t in stats]
        top = jnp.maximum(jnp.maximum(peaks[0], peaks[1]), jnp.maximum(peaks[2], peaks[3]))
        total = jnp.zeros((GROUP, DIM), jnp.float32)
        value = jnp.zeros((GROUP, DIM), jnp.float32)
        for a, peak, t in zip(at, peaks, totals):
            weight = jnp.exp2((peak - top) * SCALE)
            total = total + weight * t
            value = value + weight * o_in[a, s * GROUP:(s + 1) * GROUP, :].astype(jnp.float32)
        fin[p] = (value / total).astype(jnp.bfloat16)

    for r in range(ROWS):
        fx[r] = fin[meta_s[2, ROWS + r]]

    def r_copy(d):
        rows = pl.ds(pl.multiple_of(lax.rem(x + d, NX) * OWN, OWN), OWN)
        heads = pl.ds(pl.multiple_of(x * GROUP, GROUP), GROUP)
        if d == 0:
            return pltpu.make_async_copy(fx.at[rows], out_ref.at[:, heads, :], own_sem.at[3])
        return remote(fx.at[rows], out_ref.at[:, heads, :], r_send.at[d], r_recv.at[d], x_dev[d])

    for d in (2, 1, 3, 0):
        r_copy(d).start()
    for d in (1, 2, 3):
        x_copy(d).wait_send()
    for side in (0, 1):
        for part in (0, 1):
            first_kv(side, part).wait_send()
            for hop in range(2, FAR + (1 if side == part else 0)):
                kv_copy(side, part, hop).wait_send()
        for hop in range(1, FAR + 1 - side):
            ln_copy(side, hop).wait_send()
    for j in range(1, PLANE):
        for copy in q_copies(j):
            copy.wait_send()
        for hop in range(FAR + 1):
            for copy in back_copies(j, hop, 2 if hop < FAR else 1):
                copy.wait_send()
    r_copy(0).wait()
    for d in (1, 3, 2):
        r_copy(d).wait()


def plan(paths):
    node, row = lax.axis_index("node"), jnp.arange(ROWS, dtype=jnp.int32)
    core, z, y = lax.rem(node, NC), lax.rem(node // NC, NZ), node // (NC * NZ)
    key = paths[:, 0] * ROWS + row
    place = jnp.sum((key[None, :] < key[:, None]).astype(jnp.int32), axis=1)
    at = (place[None, :] == row[:, None]).astype(jnp.int32)
    order = jnp.sum(at * row[None, :], axis=1)
    ordered = jnp.sum(at[:, :, None] * paths[None, :, :], axis=1)
    nodes = jnp.arange(PLANE * NZ, dtype=jnp.int32)
    pair = jnp.max(jnp.where(ordered[:, :, None] == nodes, (row // 2)[:, None, None], 0), axis=(0, 1))
    its_core, its_z, its_y = lax.rem(ordered, NC), lax.rem(ordered // NC, NZ), ordered // (NC * NZ)
    partner = lax.rem(its_y - y + NY, NY) * NC + lax.rem(its_core + core, NC)
    hop = lax.rem(z - its_z + NZ, NZ)
    visit = partner * PER + jnp.where(hop <= FAR, 2 * hop, 2 * (NZ - hop) + 1)
    spare = jnp.zeros((DIM - 2 * ROWS,), jnp.int32)
    table = jnp.stack([pair, visit.reshape(-1), jnp.concatenate([order, place, spare])])
    return jnp.concatenate([table, jnp.zeros((5, DIM), jnp.int32)], axis=0)


def shards(queries, kv_cache, node_len, paths):
    rows, width = queries.shape
    meta = plan(paths)
    bf16, f32, i32 = jnp.bfloat16, jnp.float32, jnp.int32
    dma = pltpu.SemaphoreType.DMA
    vmem, smem = pl.BlockSpec(memory_space=pltpu.VMEM), pl.BlockSpec(memory_space=pltpu.SMEM)
    out = pl.pallas_call(
        kernel,
        out_shape=jax.ShapeDtypeStruct((OWN, NX * GROUP, DIM), bf16),
        in_specs=[vmem, pl.BlockSpec(memory_space=pl.ANY), vmem, smem, smem],
        out_specs=vmem,
        scratch_shapes=[
            pltpu.VMEM((ROWS, GROUP, DIM), bf16),
            pltpu.VMEM((PLANE, PAIRS, PAIR, DIM), bf16),
            pltpu.VMEM((NZ, 2, TOKENS, DIM), bf16),
            pltpu.VMEM((NZ, SUB, DIM), i32),
            pltpu.VMEM((PLANE, SUB, DIM), i32),
            pltpu.SMEM((PLANE, SUB, DIM), i32),
            pltpu.VMEM((PLANE * PER, PAIR, DIM), bf16),
            pltpu.VMEM((PLANE * PER, PAIR, DIM), bf16),
            pltpu.VMEM((PLANE * PER, SUB, DIM), f32),
            pltpu.VMEM((PLANE * PER, SUB, DIM), f32),
            pltpu.VMEM((ROWS, GROUP, DIM), bf16),
            pltpu.VMEM((ROWS, GROUP, DIM), bf16),
            dma((NX,)), dma((NX,)),
            dma((2, 2, FAR)), dma((2, 2, FAR)),
            dma((2, FAR)), dma((2, FAR)),
            dma((PLANE,)), dma((PLANE,)),
            dma((PLANE,)), dma((PLANE,)),
            dma((PLANE,)),
            dma((PLANE, FAR + 1)), dma((PLANE, FAR + 1)),
            dma((PLANE, FAR + 1)), dma((PLANE, FAR + 1)),
            dma((NX,)), dma((NX,)),
            dma((4,)),
        ],
        compiler_params=pltpu.CompilerParams(
            collective_id=0, has_side_effects=True, vmem_limit_bytes=40 * 1024 * 1024),
        cost_estimate=pl.CostEstimate(flops=1 << 30, bytes_accessed=1 << 22, transcendentals=1 << 21),
    )(queries.reshape(rows, NX * GROUP, DIM), kv_cache, meta, meta, node_len)
    return out.reshape(rows, width)


def solution(mesh):
    return jax.shard_map(
        shards,
        mesh=mesh,
        in_specs=(
            P(("node", "head"), None),
            P(None, "node", None, "head"),
            P("node"),
            P("node", None),
        ),
        out_specs=P(("node", "head"), None),
        check_vma=False,
    )
```

time: 232 us -> 78.7 us (0.34); the launches traced: 229 us -> 78.5 us
  waiting for transfers between devices: 143 us -> 0 us
  Pallas kernels: 0 us -> 73 us
  starting transfers between devices: 48.7 us -> 0 us
  local copies, waits for them, and re-layouts: 12.4 us -> 1.95 us
  other arithmetic: 11.2 us -> 2.79 us
  blocking collectives: 7.21 us -> 0 us
  matrix products: 5.89 us -> 0 us
    all_to_all x5 -> x0, waiting for transfers between devices: 143 us -> none  [the longest x1 54.3 us: shards(): lax.all_to_all(outgoing, 'node', split_axis=0, concat_axis=0, tiled=True)]
    pallas_call x0 -> x1, Pallas kernels: none -> 73 us  [shards(): pl.pallas_call(kernel, out_shape=jax.ShapeDtypeStruct((OWN, NX * GROUP, D...]
    all_to_all x5 -> x0, starting transfers between devices: 48.7 us -> none  [the longest x1 21.3 us: shards(): lax.all_to_all(outgoing, 'node', split_axis=0, concat_axis=0, tiled=True)]
    all_to_all x1 -> x0, blocking collectives: 7.21 us -> none  [shards(): lax.all_to_all(finished, 'head', split_axis=0, concat_axis=1, tiled=True)]
    dot_general x16 -> x0, matrix products: 5.89 us -> none  [the longest x8 3.31 us: attend_block(): jnp.dot(probabilities.astype(jnp.bfloat16), value_rows, preferred_element...]
    lt x9 -> x1, other arithmetic: 5.22 us -> 0.69 us  [plan(): place = jnp.sum((key[None, :] < key[:, None]).astype(jnp.int32), axis=1)]
    reshape x5 -> x0, local copies, waits for them, and re-layouts: 4.24 us -> none  [the longest x1 1.14 us: node_partials(): partial_value.reshape(n_src, slot_count, row_width)]
    gather x5 -> x0, local copies, waits for them, and re-layouts: 4.07 us -> none  [the longest x2 2.07 us: fill_slots(): picked = source[jnp.where(in_use, slot_entry // level_count, 0)]]
  transfers between devices with their start and end apart: 5 -> 0, of which waited for: 5 -> 0; matrix products, arithmetic and copies ran while one was open for 2% -> 0% of each run, Pallas kernels for 0% -> 0%
where the time goes in v2:
time: 78.7 us; the launch traced here: 78.5 us
  Pallas kernels  73 us (93%)
  other arithmetic  2.79 us (4%)
  local copies, waits for them, and re-layouts  1.95 us (2%)
    pallas_call x1, Pallas kernels, shards(): pl.pallas_call(kernel, out_shape=jax.ShapeDtypeStruct((OWN, NX * GROUP, D...  73 us
    unnamed x4, local copies, waits for them, and re-layouts  1.67 us

profile of v2, /device:TPU:1, one launch (start us, length us, event | category | flops | bytes accessed | tf_op | source)
XLA Modules:
  0.0 78.5 jit_solution(6637903171625328217)
XLA Ops:
  0.0 0.0 copy-start
  0.7 0.7 add_bitcast_fusion.1
  1.4 0.7 bitcast_add_fusion
  2.1 0.2 convert_reduce_fusion
  2.3 0.1 select_reduce_fusion.1
  2.4 0.1 add_bitcast_fusion
  2.5 0.1 pad.3.clone
  2.5 0.8 %multiply_reduce_fusion = s32[32,4]{0,1:T(4,128)S(1)} fusion(s32[32,4]{0,1:T(4,128)} %param.7, s32[32,32]{1,0:T(8,128)S(1)} %fusion), kind=kLoop, calls=%fused_computation.4 | loop fusion | flops 8064 | bytes 5120 | tf_op jit(solution)/shard_map/reduce_sum | solution.py:260
  3.4 0.1 select_reduce_fusion
  3.5 0.1 copy.7
  3.6 0.1 reduce_sum.31
  3.7 0.1 add_add_fusion.meta_ref.meta_s
  3.8 0.9 %copy.13 = bf16[1,8,64,128]{3,2,1,0:T(8,128)(2,1)S(1)} copy(bf16[1,8,64,128]{3,1,2,0:T(8,128)(2,1)} %bitcast.17) | data formatting | bytes 262144
  4.7 0.0 copy-done
  4.7 73.0 %shard_map.46 = bf16[8,64,128]{2,1,0:T(8,128)(2,1)S(1)} custom-call(bf16[8,64,128]{2,1,0:T(8,128)(2,1)S(1)} %bitcast.16, bf16[2,1,512,128]{3,2,1,0:T(8,128)(2,1)S(1)} %copy-done, s32[8,128]{1,0:T(8,128)S(1)} %add_add_fusion.meta_ref.meta_s, s32[8,128]{1,0:T(8,128)S(1)} %add_add_fusion.meta_ref.meta_s, s32[1]{0:T(128)S(6)} %copy.14.len_s), custom_call_target="tpu_custom_call" | custom-call | flops 1073741824 | bytes 4194304 | tf_op jit(solution)/shard_map/pallas_call | solution.py:278
  77.7 0.7 copy.12
  (5 shorter events, 0.0 us)
Async XLA Ops:
  0.0 4.7 %copy-start = (bf16[2,1,512,128]{3,2,1,0:T(8,128)(2,1)S(1)}, bf16[2,1,512,128]{3,2,1,0:T(8,128)(2,1)}, u32[]{:S(2)}) copy-start(bf16[2,1,512,128]{3,2,1,0:T(8,128)(2,1)} %kv_ref.1) | copy-start | bytes 786436

commit v3 on v0

v3 whole, which is shorter than its diff:
```python
import math

import jax
import jax.numpy as jnp
from jax import lax
from jax.experimental import pallas as pl
from jax.experimental.pallas import tpu as pltpu
from jax.sharding import PartitionSpec as P

MESH = pl.DeviceIdType.MESH
NX, NY, NZ, NC = 4, 4, 16, 2
PLANE = NY * NC
FAR = NZ // 2
ROWS, GROUP, DIM, TOKENS, DEPTH = 32, 16, 128, 512, 4
PAIRS = ROWS // 2
PAIR = 2 * GROUP
OWN = ROWS // NX
LANES = GROUP * DIM
SUB = 8
EMPTY = -1e30
SCALE = math.log2(math.e) / math.sqrt(DIM)
CHUNKS = 4
CHUNK = 2 * TOKENS // CHUNKS
HEAD = 16
WARM = 3
BATCH = 4
SPAN = PLANE * BATCH


def ring_slot(side, hop):
    return hop if side == 0 else lax.rem(NZ - hop, NZ)


def reach(side, chunk):
    return FAR if side == chunk % 2 else FAR - 1


def chunk_rows(chunk):
    if isinstance(chunk, int) and chunk == 0:
        return pl.ds(0, HEAD + CHUNK)
    return pl.ds(pl.multiple_of(HEAD + chunk * CHUNK, 16), CHUNK)


def kernel(
    q_ref, kv_ref, len_ref, paths_ref, out_ref,
    qx, qf, qn, qplane, kvz, len_v, paths_v, metav, metas, o_out, o_in, s_out, s_in, ff, fx,
    x_send, x_recv, kv_send, kv_recv, q_send, q_recv, m_send, m_recv,
    o_send, o_recv, s_send, s_recv, r_send, r_recv, own_sem,
):
    node = lax.axis_index("node")
    x = lax.axis_index("head")
    core = lax.rem(node, NC)
    z = lax.rem(node // NC, NZ)
    y = node // (NC * NZ)

    def dev(yy, zz, cc, xx):
        return ((yy * NZ + zz) * NC + cc, xx)

    z_dev = (dev(y, lax.rem(z + 1, NZ), core, x), dev(y, lax.rem(z + NZ - 1, NZ), core, x))
    x_dev = [None] + [dev(y, z, core, lax.rem(x + d, NX)) for d in range(1, NX)]
    p_dev = [dev(lax.rem(y + j // NC, NY), z, lax.rem(core + j % NC, NC), x) for j in range(PLANE)]
    b_dev = [dev(lax.rem(y + NY - j // NC, NY), z, lax.rem(core + j % NC, NC), x) for j in range(PLANE)]

    barrier = pltpu.get_barrier_semaphore()
    partners = list(z_dev) + x_dev[1:] + p_dev[1:]
    for partner in partners:
        pl.semaphore_signal(barrier, inc=1, device_id=partner, device_id_type=MESH)

    kv_own = [pltpu.make_async_copy(kv_ref.at[part, 0], kvz.at[0, pl.ds(HEAD + part * TOKENS, TOKENS)],
                                    own_sem.at[part]) for part in (0, 1)]
    small = [pltpu.make_async_copy(len_ref, len_v, own_sem.at[2]),
             pltpu.make_async_copy(paths_ref, paths_v, own_sem.at[3])]
    for copy in kv_own + small:
        copy.start()
    small[0].wait()
    length = jnp.broadcast_to(len_v[...], (HEAD, DIM))
    upper = lax.broadcasted_iota(jnp.int32, (HEAD, DIM), 0) < HEAD // 2
    kvz[0, 0:HEAD, :] = jnp.where(upper, length >> 8, length & 255).astype(jnp.float32).astype(jnp.bfloat16)
    for copy in kv_own:
        copy.wait()
    pl.semaphore_wait(barrier, len(partners))

    def remote(src, dst, send, recv, to):
        return pltpu.make_async_remote_copy(
            src_ref=src, dst_ref=dst, send_sem=send, recv_sem=recv, device_id=to, device_id_type=MESH)

    def kv_copy(side, chunk, hop):
        rows = chunk_rows(chunk)
        return remote(kvz.at[ring_slot(side, hop - 1), rows], kvz.at[ring_slot(side, hop), rows],
                      kv_send.at[side, chunk], kv_recv.at[side, chunk, hop - 1], z_dev[side])

    def x_copy(d):
        lanes = pl.ds(pl.multiple_of(lax.rem(x + d, NX) * LANES, LANES), LANES)
        if d == 0:
            return pltpu.make_async_copy(q_ref.at[:, lanes], qx.at[x], x_recv.at[0])
        return remote(q_ref.at[:, lanes], qx.at[x], x_send.at[0], x_recv.at[d], x_dev[d])

    for side in (0, 1):
        kv_copy(side, 0, 1).start()
    for d in (2, 1, 3, 0):
        x_copy(d).start()
    for chunk in range(1, CHUNKS):
        for side in (0, 1):
            kv_copy(side, chunk, 1).start()

    def relay(hop, chunk, far=False):
        for side in (0, 1):
            last = reach(side, chunk) if far else FAR
            if not far or hop <= last:
                kv_copy(side, chunk, hop).wait_recv()
            if not far or hop < last:
                kv_copy(side, chunk, hop).wait_send()
                kv_copy(side, chunk, hop + 1).start()

    small[1].wait()
    row = lax.broadcasted_iota(jnp.int32, (ROWS, DIM), 0)
    col = lax.broadcasted_iota(jnp.int32, (ROWS, DIM), 1)

    def upright(line):
        return jnp.sum(jnp.where(row == col, line, 0), axis=1, keepdims=True)

    wide = jnp.concatenate([paths_v[...], jnp.zeros((DEPTH, DIM - ROWS), jnp.int32)], axis=1)
    key_line = wide[0:1, :] * ROWS + col[0:1, :]
    key = upright(key_line)
    place_line = jnp.sum(jnp.where(key < key_line, 1, 0), axis=0, keepdims=True)
    place = upright(place_line)
    order_line = jnp.sum(jnp.where(place == col, row, 0), axis=0, keepdims=True)
    pair = jnp.zeros((ROWS, DIM), jnp.int32)
    for j in range(DEPTH):
        pair = jnp.maximum(pair, jnp.where(upright(wide[j:j + 1, :]) == col, place >> 1, 0))
    metav[0, 0:1, :] = jnp.max(pair, axis=0, keepdims=True)
    for j in range(DEPTH):
        n = wide[j:j + 1, :]
        partner = (((n >> 5) - y + NY) & (NY - 1)) * NC + (((n & 1) + core) & 1)
        hop = (z - ((n >> 1) & (NZ - 1)) + NZ) & (NZ - 1)
        t = jnp.where(hop == 0, 0, jnp.where(hop <= FAR, 2 * hop - 1, 2 * (NZ - hop)))
        at = (t >> 2) * SPAN + partner * BATCH + (t & 3)
        metav[0, 1 + j:2 + j, :] = at * 2 + (place_line & 1)
    metav[0, 5:6, :] = order_line
    metav[0, 6:8, :] = jnp.zeros((2, DIM), jnp.int32)
    own_meta = pltpu.make_async_copy(metav.at[0], metas.at[0], own_sem.at[4])
    own_meta.start()

    relay(1, 0)
    x_copy(0).wait()
    for d in (1, 3, 2):
        x_copy(d).wait_recv()
    for h in range(GROUP):
        for i in range(NX):
            qf[h * ROWS + i * OWN:h * ROWS + (i + 1) * OWN, :] = (
                qx[i, :, h * DIM:(h + 1) * DIM].astype(jnp.float32))
    relay(1, 1)
    for r in range(ROWS):
        qn[r] = qf[pl.ds(r, GROUP, stride=ROWS), :].astype(jnp.bfloat16)
    own_meta.wait()
    for p in range(ROWS):
        qplane[0, p // 2, (p % 2) * GROUP:(p % 2 + 1) * GROUP, :] = qn[metas[0, 5, p]]

    def q_copies(j, count=1):
        src = pl.ds(0, count)
        return (
            remote(qplane.at[src], qplane.at[pl.ds(j, count)], q_send.at[0], q_recv.at[0], p_dev[j]),
            remote(metav.at[src], metav.at[pl.ds(j, count)], m_send.at[0], m_recv.at[0], p_dev[j]),
        )

    for j in (4, 5, 2, 3, 6, 7, 1):
        for copy in q_copies(j):
            copy.start()

    lane = lax.broadcasted_iota(jnp.int32, (SUB, DIM), 1)
    token = lax.broadcasted_iota(jnp.int32, (1, TOKENS), 1).astype(jnp.float32)

    def ring_of(t):
        odd = lax.rem(t, 2)
        return odd * ((t + 1) // 2) + (1 - odd) * lax.rem(NZ - t // 2, NZ)

    def scores(t, j0):
        i = ring_of(t)
        n = (y * NZ + lax.rem(z + NZ - i, NZ)) * NC + core
        head = kvz[i, 0:HEAD, :].astype(jnp.float32)
        length = head[0:1, :] * 256.0 + head[HEAD // 2:HEAD // 2 + 1, :]
        bias = jnp.where(token < jnp.concatenate([length] * (TOKENS // DIM), axis=1), 0.0, EMPTY)
        lhs = jnp.concatenate([qplane[j, metas[j, 0, n]] for j in range(j0, j0 + 4)], axis=0)
        score = lax.dot_general(lhs, kvz[i, pl.ds(HEAD, TOKENS), :], (((1,), (1,)), ((), ())),
                                preferred_element_type=jnp.float32) + bias
        peak = jnp.max(score, axis=1, keepdims=True)
        prob = jnp.exp2((score - peak) * SCALE)
        return prob.astype(jnp.bfloat16), peak, jnp.sum(prob, axis=1, keepdims=True)

    def values(t, j0, prob, peak, total):
        i = ring_of(t)
        value = jnp.dot(prob, kvz[i, pl.ds(HEAD + TOKENS, TOKENS), :],
                        preferred_element_type=jnp.float32).astype(jnp.bfloat16)
        for j in range(j0, j0 + 4):
            base = (j - j0) * PAIR
            at = t // BATCH * SPAN + j * BATCH + lax.rem(t, BATCH)
            stat = jnp.zeros((SUB, DIM), jnp.float32)
            for c in range(PAIR // SUB):
                rows = slice(base + c * SUB, base + (c + 1) * SUB)
                stat = jnp.where(lane == c, peak[rows], stat)
                stat = jnp.where(lane == c + PAIR // SUB, total[rows], stat)
            for c in range(2):
                (o_in if j == 0 else o_out)[2 * at + c] = value[base + c * GROUP:base + (c + 1) * GROUP]
            (s_in if j == 0 else s_out)[at] = stat

    def attend(t):
        for j0 in (0, 4):
            values(t, j0, *scores(t, j0))

    def back_copies(j, b, first, count):
        at = pl.ds(b * SPAN + j * BATCH + first, count)
        both = pl.ds(2 * (b * SPAN + j * BATCH + first), 2 * count)
        return (
            remote(o_out.at[both], o_in.at[both], o_send.at[b], o_recv.at[b], b_dev[j]),
            remote(s_out.at[at], s_in.at[at], s_send.at[b], s_recv.at[b], b_dev[j]),
        )

    def send(b, first, count, partners=range(1, PLANE)):
        for j in partners:
            for copy in back_copies(j, b, first, count):
                copy.start()

    def all_copies(b):
        return back_copies(1, b, 0, SPAN - BATCH)

    for chunk in range(2, CHUNKS):
        relay(1, chunk)
    for hop in range(2, WARM + 1):
        for chunk in range(CHUNKS):
            relay(hop, chunk)
    for copy in q_copies(1, PLANE - 1):
        copy.wait_recv()
    all_meta = pltpu.make_async_copy(metav.at[pl.ds(1, PLANE - 1)], metas.at[pl.ds(1, PLANE - 1)], own_sem.at[5])
    all_meta.start()
    all_meta.wait()

    def one_hop(b, carry):
        hop = WARM + 1 + b

        def one_chunk(chunk, carry):
            @pl.when(chunk == 0)
            def _():
                relay(hop, 0)

            @pl.when(chunk > 0)
            def _():
                relay(hop, chunk)

            attend(BATCH * b + chunk)
            return carry

        lax.fori_loop(0, CHUNKS, one_chunk, 0)
        send(b, 0, BATCH)

        @pl.when(b >= 1)
        def _():
            for copy in all_copies(b - 1):
                copy.wait()

        return carry

    lax.fori_loop(0, 3, one_hop, 0)
    for chunk in range(CHUNKS):
        relay(FAR - 1, chunk, True)
        if chunk == 0:
            attend(12)
            for copy in all_copies(2):
                copy.wait()
    attend(13)
    relay(FAR, 0, True)
    attend(14)
    send(3, 0, 3)
    relay(FAR, 1, True)
    last = [(j0, scores(15, j0)) for j0 in (4, 0)]
    relay(FAR, 2, True)
    relay(FAR, 3, True)
    for j0, found in last:
        values(15, j0, *found)
        send(3, 3, 1, range(max(j0, 1), j0 + 4))
    for copy in all_copies(3):
        copy.wait_recv()

    def finish(r):
        at = [metas[0, 1 + j, r] for j in range(DEPTH)]
        stats = []
        for a in at:
            tile = s_in[a // 2]
            stats.append(jnp.where(a % 2 == 1, pltpu.roll(tile, DIM - 2, 1), tile))
        top = jnp.maximum(jnp.maximum(stats[0], stats[1]), jnp.maximum(stats[2], stats[3]))
        weight = [jnp.exp2((t - top) * SCALE) for t in stats]
        total = sum(pltpu.roll(w, PAIR // SUB, 1) * t for w, t in zip(weight, stats))
        share = pltpu.roll(1.0 / jnp.where(lane < PAIR // SUB, 1.0, total), DIM - PAIR // SUB, 1)
        value = jnp.zeros((GROUP, DIM), jnp.float32)
        for a, w in zip(at, weight):
            w = w * share
            w = jnp.concatenate([jnp.broadcast_to(w[:, c:c + 1], (SUB, DIM)) for c in range(GROUP // SUB)], axis=0)
            value = value + w * o_in[a].astype(jnp.float32)
        return value

    def r_copy(d):
        lanes = pl.ds(pl.multiple_of(x * LANES, LANES), LANES)
        if d == 0:
            return pltpu.make_async_copy(fx.at[0], out_ref.at[:, lanes], r_recv.at[0])
        return remote(fx.at[d], out_ref.at[:, lanes], r_send.at[0], r_recv.at[d], x_dev[d])

    for d in (2, 1, 3, 0):
        for r in range(OWN):
            ff[d, pl.ds(r, GROUP, stride=OWN), :] = finish(lax.rem(x + d, NX) * OWN + r)
        for h in range(GROUP):
            fx[d, :, h * DIM:(h + 1) * DIM] = ff[d, h * OWN:(h + 1) * OWN, :].astype(jnp.bfloat16)
        r_copy(d).start()
    for d in (1, 2, 3):
        x_copy(d).wait_send()
    for side in (0, 1):
        for chunk in range(CHUNKS):
            kv_copy(side, chunk, reach(side, chunk)).wait_send()
    for copy in q_copies(1, PLANE - 1) + all_copies(3):
        copy.wait_send()
    r_copy(0).wait()
    for d in (1, 3, 2):
        r_copy(d).wait()


def shards(queries, kv_cache, node_len, paths):
    rows, width = queries.shape
    bf16, f32, i32 = jnp.bfloat16, jnp.float32, jnp.int32
    dma = pltpu.SemaphoreType.DMA
    anywhere = pl.BlockSpec(memory_space=pl.ANY)
    return pl.pallas_call(
        kernel,
        out_shape=jax.ShapeDtypeStruct((rows, width), bf16),
        in_specs=[anywhere] * 4,
        out_specs=anywhere,
        scratch_shapes=[
            pltpu.VMEM((NX, OWN, LANES), bf16),
            pltpu.VMEM((GROUP * ROWS, DIM), f32),
            pltpu.VMEM((ROWS, GROUP, DIM), bf16),
            pltpu.VMEM((PLANE, PAIRS, PAIR, DIM), bf16),
            pltpu.VMEM((NZ, HEAD + 2 * TOKENS, DIM), bf16),
            pltpu.VMEM((1, 1), i32),
            pltpu.VMEM((DEPTH, ROWS), i32),
            pltpu.VMEM((PLANE, SUB, DIM), i32),
            pltpu.SMEM((PLANE, SUB, DIM), i32),
            pltpu.VMEM((2 * PLANE * NZ, GROUP, DIM), bf16),
            pltpu.VMEM((2 * PLANE * NZ, GROUP, DIM), bf16),
            pltpu.VMEM((PLANE * NZ, SUB, DIM), f32),
            pltpu.VMEM((PLANE * NZ, SUB, DIM), f32),
            pltpu.VMEM((NX, GROUP * OWN, DIM), f32),
            pltpu.VMEM((NX, OWN, LANES), bf16),
            dma((1,)), dma((NX,)),
            dma((2, CHUNKS)), dma((2, CHUNKS, FAR)),
            dma((1,)), dma((1,)),
            dma((1,)), dma((1,)),
            dma((NZ // BATCH,)), dma((NZ // BATCH,)),
            dma((NZ // BATCH,)), dma((NZ // BATCH,)),
            dma((1,)), dma((NX,)),
            dma((6,)),
        ],
        compiler_params=pltpu.CompilerParams(
            collective_id=0, has_side_effects=True, vmem_limit_bytes=60 * 1024 * 1024),
        cost_estimate=pl.CostEstimate(flops=1 << 30, bytes_accessed=1 << 22, transcendentals=1 << 21),
    )(queries, kv_cache, node_len.reshape(1, 1), paths.T)


def solution(mesh):
    return jax.shard_map(
        shards,
        mesh=mesh,
        in_specs=(
            P(("node", "head"), None),
            P(None, "node", None, "head"),
            P("node"),
            P("node", None),
        ),
        out_specs=P(("node", "head"), None),
        check_vma=False,
    )
```

time: 232 us -> 73.3 us (0.32); the launches traced: 229 us -> 73.2 us
  waiting for transfers between devices: 143 us -> 0 us
  Pallas kernels: 0 us -> 70.9 us
  starting transfers between devices: 48.7 us -> 0 us
  other arithmetic: 11.2 us -> 0 us
  local copies, waits for them, and re-layouts: 12.4 us -> 1.57 us
  blocking collectives: 7.21 us -> 0 us
  matrix products: 5.89 us -> 0 us
    all_to_all x5 -> x0, waiting for transfers between devices: 143 us -> none  [the longest x1 54.3 us: shards(): lax.all_to_all(outgoing, 'node', split_axis=0, concat_axis=0, tiled=True)]
    pallas_call x0 -> x1, Pallas kernels: none -> 70.9 us  [shards(): pl.pallas_call(kernel, out_shape=jax.ShapeDtypeStruct((rows, width), bf16...]
    all_to_all x5 -> x0, starting transfers between devices: 48.7 us -> none  [the longest x1 21.3 us: shards(): lax.all_to_all(outgoing, 'node', split_axis=0, concat_axis=0, tiled=True)]
    all_to_all x1 -> x0, blocking collectives: 7.21 us -> none  [shards(): lax.all_to_all(finished, 'head', split_axis=0, concat_axis=1, tiled=True)]
    dot_general x16 -> x0, matrix products: 5.89 us -> none  [the longest x8 3.31 us: attend_block(): jnp.dot(probabilities.astype(jnp.bfloat16), value_rows, preferred_element...]
    lt x9 -> x0, other arithmetic: 5.22 us -> none  [the longest x8 5.22 us: node_partials(): in_range = jnp.arange(key_rows.shape[0], dtype=jnp.int32) < length]
    reshape x5 -> x0, local copies, waits for them, and re-layouts: 4.24 us -> none  [the longest x1 1.14 us: node_partials(): partial_value.reshape(n_src, slot_count, row_width)]
    gather x5 -> x0, local copies, waits for them, and re-layouts: 4.07 us -> none  [the longest x2 2.07 us: fill_slots(): picked = source[jnp.where(in_use, slot_entry // level_count, 0)]]
  transfers between devices with their start and end apart: 5 -> 0, of which waited for: 5 -> 0; matrix products, arithmetic and copies ran while one was open for 2% -> 0% of each run, Pallas kernels for 0% -> 0%
where the time goes in v3:
time: 73.3 us; the launch traced here: 73.2 us
  Pallas kernels  70.9 us (97%)
  local copies, waits for them, and re-layouts  1.57 us (2%)
    pallas_call x1, Pallas kernels, shards(): pl.pallas_call(kernel, out_shape=jax.ShapeDtypeStruct((rows, width), bf16...  70.9 us
    unnamed x1, local copies, waits for them, and re-layouts  1.57 us

profile of v3, /device:TPU:1, one launch (start us, length us, event | category | flops | bytes accessed | tf_op | source)
XLA Modules:
  0.0 73.2 jit_solution(9186560499366160840)
XLA Ops:
  0.7 70.9 %shard_map.46 = bf16[8,8192]{1,0:T(8,128)(2,1)} custom-call(bf16[8,8192]{1,0:T(8,128)(2,1)} %q_ref.1, bf16[2,1,512,128]{3,2,1,0:T(8,128)(2,1)} %kv_ref.1, s32[1,1]{1,0:T(1,128)} %bitcast.2.len_ref, s32[4,32]{1,0:T(4,128)} %bitcast.3), custom_call_target="tpu_custom_call" | custom-call | flops 1073741824 | bytes 4194304 | tf_op jit(solution)/shard_map/pallas_call | solution.py:329
  71.6 1.6 %copy.7 = bf16[8,8192]{1,0:T(8,128)(2,1)} copy(bf16[8,8192]{1,0:T(8,128)(2,1)} %shard_map.46) | data formatting | bytes 262144

commit v4 on v3

--- a/solution.py
+++ b/solution.py
@@ -119,18 +119,18 @@
     def upright(line):
         return jnp.sum(jnp.where(row == col, line, 0), axis=1, keepdims=True)
 
-    wide = jnp.concatenate([paths_v[...], jnp.zeros((DEPTH, DIM - ROWS), jnp.int32)], axis=1)
-    key_line = wide[0:1, :] * ROWS + col[0:1, :]
-    key = upright(key_line)
+    level = [paths_v[:, j:j + 1] for j in range(DEPTH)]
+    key = level[0] * ROWS + row[:, 0:1]
+    key_line = jnp.sum(jnp.where(row == col, key, 0), axis=0, keepdims=True)
     place_line = jnp.sum(jnp.where(key < key_line, 1, 0), axis=0, keepdims=True)
     place = upright(place_line)
     order_line = jnp.sum(jnp.where(place == col, row, 0), axis=0, keepdims=True)
     pair = jnp.zeros((ROWS, DIM), jnp.int32)
     for j in range(DEPTH):
-        pair = jnp.maximum(pair, jnp.where(upright(wide[j:j + 1, :]) == col, place >> 1, 0))
+        pair = jnp.maximum(pair, jnp.where(level[j] == col, place >> 1, 0))
     metav[0, 0:1, :] = jnp.max(pair, axis=0, keepdims=True)
     for j in range(DEPTH):
-        n = wide[j:j + 1, :]
+        n = jnp.sum(jnp.where(row == col, level[j], 0), axis=0, keepdims=True)
         partner = (((n >> 5) - y + NY) & (NY - 1)) * NC + (((n & 1) + core) & 1)
         hop = (z - ((n >> 1) & (NZ - 1)) + NZ) & (NZ - 1)
         t = jnp.where(hop == 0, 0, jnp.where(hop <= FAR, 2 * hop - 1, 2 * (NZ - hop)))
@@ -228,6 +228,7 @@
     for hop in range(2, WARM + 1):
         for chunk in range(CHUNKS):
             relay(hop, chunk)
+    relay(WARM + 1, 0)
     for copy in q_copies(1, PLANE - 1):
         copy.wait_recv()
     all_meta = pltpu.make_async_copy(metav.at[pl.ds(1, PLANE - 1)], metas.at[pl.ds(1, PLANE - 1)], own_sem.at[5])
@@ -237,46 +238,45 @@
     def one_hop(b, carry):
         hop = WARM + 1 + b
 
-        def one_chunk(chunk, carry):
-            @pl.when(chunk == 0)
+        def one_chunk(q, carry):
+            @pl.when((q >= 1) & (q < CHUNKS))
             def _():
-                relay(hop, 0)
-
-            @pl.when(chunk > 0)
-            def _():
-                relay(hop, chunk)
-
-            attend(BATCH * b + chunk)
+                relay(hop, q)
+
+            attend(BATCH * b + q)
             return carry
 
         lax.fori_loop(0, CHUNKS, one_chunk, 0)
+
+        @pl.when(b < 2)
+        def _():
+            relay(hop + 1, 0)
+
         send(b, 0, BATCH)
 
-        @pl.when(b >= 1)
-        def _():
-            for copy in all_copies(b - 1):
-                copy.wait()
-
         return carry
 
     lax.fori_loop(0, 3, one_hop, 0)
-    for chunk in range(CHUNKS):
-        relay(FAR - 1, chunk, True)
-        if chunk == 0:
-            attend(12)
-            for copy in all_copies(2):
-                copy.wait()
-    attend(13)
+    relay(FAR - 1, 0, True)
+    attend(12)
+    relay(FAR - 1, 1, True)
+    found = [(t, j0, scores(t, j0)) for t in (13, 14) for j0 in (0, 4)]
+    relay(FAR - 1, 2, True)
+    relay(FAR - 1, 3, True)
+    for t, j0, parts in found:
+        values(t, j0, *parts)
+    send(3, 0, 3)
     relay(FAR, 0, True)
-    attend(14)
-    send(3, 0, 3)
     relay(FAR, 1, True)
-    last = [(j0, scores(15, j0)) for j0 in (4, 0)]
+    found = [(j0, scores(15, j0)) for j0 in (4, 0)]
     relay(FAR, 2, True)
     relay(FAR, 3, True)
-    for j0, found in last:
-        values(15, j0, *found)
+    for j0, parts in found:
+        values(15, j0, *parts)
         send(3, 3, 1, range(max(j0, 1), j0 + 4))
+    for b in range(3):
+        for copy in all_copies(b):
+            copy.wait()
     for copy in all_copies(3):
         copy.wait_recv()
 
@@ -338,7 +338,7 @@
             pltpu.VMEM((PLANE, PAIRS, PAIR, DIM), bf16),
             pltpu.VMEM((NZ, HEAD + 2 * TOKENS, DIM), bf16),
             pltpu.VMEM((1, 1), i32),
-            pltpu.VMEM((DEPTH, ROWS), i32),
+            pltpu.VMEM((ROWS, DEPTH), i32),
             pltpu.VMEM((PLANE, SUB, DIM), i32),
             pltpu.SMEM((PLANE, SUB, DIM), i32),
             pltpu.VMEM((2 * PLANE * NZ, GROUP, DIM), bf16),
@@ -357,9 +357,9 @@
             dma((6,)),
         ],
         compiler_params=pltpu.CompilerParams(
-            collective_id=0, has_side_effects=True, vmem_limit_bytes=60 * 1024 * 1024),
+            collective_id=0, has_side_effects=True, vmem_limit_bytes=56356864),
         cost_estimate=pl.CostEstimate(flops=1 << 30, bytes_accessed=1 << 22, transcendentals=1 << 21),
-    )(queries, kv_cache, node_len.reshape(1, 1), paths.T)
+    )(queries, kv_cache, node_len.reshape(1, 1), paths)
 
 
 def solution(mesh):

time: 73.3 us -> 69.6 us (0.950)
  Pallas kernels: 70.9 us -> 68 us
  local copies, waits for them, and re-layouts: 1.57 us -> 0.76 us
    pallas_call x1, Pallas kernels: 70.9 us -> 68 us  [shards(): pl.pallas_call(kernel, out_shape=jax.ShapeDtypeStruct((rows, width), bf16...]
    unnamed x1 -> x4, local copies, waits for them, and re-layouts: 1.57 us -> 0.76 us
where the time goes in v4:
time: 69.6 us; the launch traced here: 69.4 us
  Pallas kernels  68 us (98%)
  local copies, waits for them, and re-layouts  0.76 us (1%)
    pallas_call x1, Pallas kernels, shards(): pl.pallas_call(kernel, out_shape=jax.ShapeDtypeStruct((rows, width), bf16...  68 us

profile of v4, /device:TPU:1, one launch (start us, length us, event | category | flops | bytes accessed | tf_op | source)
XLA Modules:
  0.0 69.4 jit_solution(4466201043781454707)
XLA Ops:
  0.0 0.0 copy-start
  0.7 0.0 copy-done
  0.7 0.1 copy.5.paths_ref
  0.8 68.0 %shard_map.46 = bf16[8,8192]{1,0:T(8,128)(2,1)S(1)} custom-call(bf16[8,8192]{1,0:T(8,128)(2,1)} %q_ref.1, bf16[2,1,512,128]{3,2,1,0:T(8,128)(2,1)} %kv_ref.1, s32[1,1]{1,0:T(1,128)} %bitcast.1.len_ref, s32[32,4]{1,0:T(8,128)S(1)} %copy.5.paths_ref), custom_call_target="tpu_custom_call" | custom-call | flops 1073741824 | bytes 4194304 | tf_op jit(solution)/shard_map/pallas_call | solution.py:329
  68.8 0.7 copy.8
Async XLA Ops:
  0.0 0.7 copy-start

commit v5 on v4

--- a/solution.py
+++ b/solution.py
@@ -95,16 +95,20 @@
             return pltpu.make_async_copy(q_ref.at[:, lanes], qx.at[x], x_recv.at[0])
         return remote(q_ref.at[:, lanes], qx.at[x], x_send.at[0], x_recv.at[d], x_dev[d])
 
+    def chunk_of(side, step):
+        return step ^ side
+
     for side in (0, 1):
-        kv_copy(side, 0, 1).start()
+        kv_copy(side, chunk_of(side, 0), 1).start()
     for d in (2, 1, 3, 0):
         x_copy(d).start()
-    for chunk in range(1, CHUNKS):
+    for step in range(1, CHUNKS):
         for side in (0, 1):
-            kv_copy(side, chunk, 1).start()
-
-    def relay(hop, chunk, far=False):
+            kv_copy(side, chunk_of(side, step), 1).start()
+
+    def relay(hop, step, far=False):
         for side in (0, 1):
+            chunk = chunk_of(side, step)
             last = reach(side, chunk) if far else FAR
             if not far or hop <= last:
                 kv_copy(side, chunk, hop).wait_recv()
@@ -239,9 +243,10 @@
         hop = WARM + 1 + b
 
         def one_chunk(q, carry):
-            @pl.when((q >= 1) & (q < CHUNKS))
-            def _():
-                relay(hop, q)
+            for step in range(1, CHUNKS):
+                @pl.when(q == step)
+                def _(step=step):
+                    relay(hop, step)
 
             attend(BATCH * b + q)
             return carry
@@ -267,10 +272,8 @@
         values(t, j0, *parts)
     send(3, 0, 3)
     relay(FAR, 0, True)
-    relay(FAR, 1, True)
     found = [(j0, scores(15, j0)) for j0 in (4, 0)]
     relay(FAR, 2, True)
-    relay(FAR, 3, True)
     for j0, parts in found:
         values(15, j0, *parts)
         send(3, 3, 1, range(max(j0, 1), j0 + 4))

time: 69.6 us -> 69.4 us (level)
  no operation moved by 1% of the time
where the time goes in v5:
time: 69.4 us; the launch traced here: 69.3 us
  Pallas kernels  67.9 us (98%)
  local copies, waits for them, and re-layouts  0.76 us (1%)
    pallas_call x1, Pallas kernels, shards(): pl.pallas_call(kernel, out_shape=jax.ShapeDtypeStruct((rows, width), bf16...  67.9 us

profile of v5, /device:TPU:1, one launch (start us, length us, event | category | flops | bytes accessed | tf_op | source)
XLA Modules:
  0.0 69.3 jit_solution(12186772861825942299)
XLA Ops:
  0.0 0.0 copy-start
  0.7 0.0 copy-done
  0.7 0.1 copy.5.paths_ref
  0.8 67.9 %shard_map.46 = bf16[8,8192]{1,0:T(8,128)(2,1)S(1)} custom-call(bf16[8,8192]{1,0:T(8,128)(2,1)} %q_ref.1, bf16[2,1,512,128]{3,2,1,0:T(8,128)(2,1)} %kv_ref.1, s32[1,1]{1,0:T(1,128)} %bitcast.1.len_ref, s32[32,4]{1,0:T(8,128)S(1)} %copy.5.paths_ref), custom_call_target="tpu_custom_call" | custom-call | flops 1073741824 | bytes 4194304 | tf_op jit(solution)/shard_map/pallas_call | solution.py:332
  68.6 0.7 copy.8
Async XLA Ops:
  0.0 0.7 copy-start

commit v6 on v5

--- a/solution.py
+++ b/solution.py
@@ -22,6 +22,7 @@
 CHUNKS = 4
 CHUNK = 2 * TOKENS // CHUNKS
 HEAD = 16
+VALUES = TOKENS + HEAD
 WARM = 3
 BATCH = 4
 SPAN = PLANE * BATCH
@@ -36,8 +37,8 @@
 
 
 def chunk_rows(chunk):
-    if isinstance(chunk, int) and chunk == 0:
-        return pl.ds(0, HEAD + CHUNK)
+    if isinstance(chunk, int):
+        return pl.ds(chunk * CHUNK + (HEAD if chunk > 1 else 0), CHUNK + (HEAD if chunk == 1 else 0))
     return pl.ds(pl.multiple_of(HEAD + chunk * CHUNK, 16), CHUNK)
 
 
@@ -66,28 +67,26 @@
     for partner in partners:
         pl.semaphore_signal(barrier, inc=1, device_id=partner, device_id_type=MESH)
 
-    kv_own = [pltpu.make_async_copy(kv_ref.at[part, 0], kvz.at[0, pl.ds(HEAD + part * TOKENS, TOKENS)],
+    kv_own = [pltpu.make_async_copy(kv_ref.at[part, 0], kvz.at[0, pl.ds(part * VALUES, TOKENS)],
                                     own_sem.at[part]) for part in (0, 1)]
     small = [pltpu.make_async_copy(len_ref, len_v, own_sem.at[2]),
              pltpu.make_async_copy(paths_ref, paths_v, own_sem.at[3])]
-    for copy in kv_own + small:
+    for copy in small + kv_own:
         copy.start()
-    small[0].wait()
-    length = jnp.broadcast_to(len_v[...], (HEAD, DIM))
-    upper = lax.broadcasted_iota(jnp.int32, (HEAD, DIM), 0) < HEAD // 2
-    kvz[0, 0:HEAD, :] = jnp.where(upper, length >> 8, length & 255).astype(jnp.float32).astype(jnp.bfloat16)
-    for copy in kv_own:
-        copy.wait()
     pl.semaphore_wait(barrier, len(partners))
 
     def remote(src, dst, send, recv, to):
         return pltpu.make_async_remote_copy(
             src_ref=src, dst_ref=dst, send_sem=send, recv_sem=recv, device_id=to, device_id_type=MESH)
 
-    def kv_copy(side, chunk, hop):
+    def kv_copy(side, chunk, hop, first=False):
         rows = chunk_rows(chunk)
+        if first:
+            src = kv_ref.at[chunk // 2, 0, pl.ds(chunk % 2 * CHUNK, CHUNK)]
+            return remote(src, kvz.at[ring_slot(side, 1), rows], kv_send.at[side, chunk],
+                          kv_recv.at[chunk ^ side, 0], z_dev[side])
         return remote(kvz.at[ring_slot(side, hop - 1), rows], kvz.at[ring_slot(side, hop), rows],
-                      kv_send.at[side, chunk], kv_recv.at[side, chunk, hop - 1], z_dev[side])
+                      kv_send.at[side, chunk], kv_recv.at[chunk ^ side, hop - 1], z_dev[side])
 
     def x_copy(d):
         lanes = pl.ds(pl.multiple_of(lax.rem(x + d, NX) * LANES, LANES), LANES)
@@ -98,22 +97,28 @@
     def chunk_of(side, step):
         return step ^ side
 
-    for side in (0, 1):
-        kv_copy(side, chunk_of(side, 0), 1).start()
+    kv_copy(0, 0, 1, True).start()
     for d in (2, 1, 3, 0):
         x_copy(d).start()
+    small[0].wait()
+    length = jnp.broadcast_to(len_v[...], (HEAD, DIM))
+    upper = lax.broadcasted_iota(jnp.int32, (HEAD, DIM), 0) < HEAD // 2
+    kvz[0, TOKENS:VALUES, :] = jnp.where(upper, length >> 8, length & 255).astype(jnp.float32).astype(jnp.bfloat16)
+    kv_own[0].wait()
+    kv_copy(1, 1, 1).start()
     for step in range(1, CHUNKS):
         for side in (0, 1):
-            kv_copy(side, chunk_of(side, step), 1).start()
+            kv_copy(side, chunk_of(side, step), 1, chunk_of(side, step) != 1).start()
 
     def relay(hop, step, far=False):
+        rows = pl.ds(0, 2 * CHUNK + (HEAD if step < 2 else 0))
+        remote(kvz.at[1, rows], kvz.at[1, rows], kv_send.at[0, 0], kv_recv.at[step, hop - 1], z_dev[0]).wait_recv()
         for side in (0, 1):
             chunk = chunk_of(side, step)
+            own = isinstance(hop, int) and hop == 1 and chunk != 1
             last = reach(side, chunk) if far else FAR
-            if not far or hop <= last:
-                kv_copy(side, chunk, hop).wait_recv()
             if not far or hop < last:
-                kv_copy(side, chunk, hop).wait_send()
+                kv_copy(side, chunk, hop, own).wait_send()
                 kv_copy(side, chunk, hop + 1).start()
 
     small[1].wait()
@@ -181,11 +186,11 @@
     def scores(t, j0):
         i = ring_of(t)
         n = (y * NZ + lax.rem(z + NZ - i, NZ)) * NC + core
-        head = kvz[i, 0:HEAD, :].astype(jnp.float32)
+        head = kvz[i, TOKENS:VALUES, :].astype(jnp.float32)
         length = head[0:1, :] * 256.0 + head[HEAD // 2:HEAD // 2 + 1, :]
         bias = jnp.where(token < jnp.concatenate([length] * (TOKENS // DIM), axis=1), 0.0, EMPTY)
         lhs = jnp.concatenate([qplane[j, metas[j, 0, n]] for j in range(j0, j0 + 4)], axis=0)
-        score = lax.dot_general(lhs, kvz[i, pl.ds(HEAD, TOKENS), :], (((1,), (1,)), ((), ())),
+        score = lax.dot_general(lhs, kvz[i, 0:TOKENS, :], (((1,), (1,)), ((), ())),
                                 preferred_element_type=jnp.float32) + bias
         peak = jnp.max(score, axis=1, keepdims=True)
         prob = jnp.exp2((score - peak) * SCALE)
@@ -193,7 +198,7 @@
 
     def values(t, j0, prob, peak, total):
         i = ring_of(t)
-        value = jnp.dot(prob, kvz[i, pl.ds(HEAD + TOKENS, TOKENS), :],
+        value = jnp.dot(prob, kvz[i, VALUES:VALUES + TOKENS, :],
                         preferred_element_type=jnp.float32).astype(jnp.bfloat16)
         for j in range(j0, j0 + 4):
             base = (j - j0) * PAIR
@@ -227,6 +232,7 @@
     def all_copies(b):
         return back_copies(1, b, 0, SPAN - BATCH)
 
+    kv_own[1].wait()
     for chunk in range(2, CHUNKS):
         relay(1, chunk)
     for hop in range(2, WARM + 1):
@@ -351,7 +357,7 @@
             pltpu.VMEM((NX, GROUP * OWN, DIM), f32),
             pltpu.VMEM((NX, OWN, LANES), bf16),
             dma((1,)), dma((NX,)),
-            dma((2, CHUNKS)), dma((2, CHUNKS, FAR)),
+            dma((2, CHUNKS)), dma((CHUNKS, FAR)),
             dma((1,)), dma((1,)),
             dma((1,)), dma((1,)),
             dma((NZ // BATCH,)), dma((NZ // BATCH,)),

time: 69.4 us -> 69.5 us (level)
  no operation moved by 1% of the time
where the time goes in v6:
time: 69.5 us; the launch traced here: 69.3 us
  Pallas kernels  67.9 us (98%)
  local copies, waits for them, and re-layouts  0.76 us (1%)
    pallas_call x1, Pallas kernels, shards(): pl.pallas_call(kernel, out_shape=jax.ShapeDtypeStruct((rows, width), bf16...  67.9 us

profile of v6, /device:TPU:1, one launch (start us, length us, event | category | flops | bytes accessed | tf_op | source)
XLA Modules:
  0.0 69.3 jit_solution(16127751837669826745)
XLA Ops:
  0.0 0.0 copy-start
  0.7 0.0 copy-done
  0.7 0.1 copy.5.paths_ref
  0.8 67.9 %shard_map.46 = bf16[8,8192]{1,0:T(8,128)(2,1)S(1)} custom-call(bf16[8,8192]{1,0:T(8,128)(2,1)} %q_ref.1, bf16[2,1,512,128]{3,2,1,0:T(8,128)(2,1)} %kv_ref.1, s32[1,1]{1,0:T(1,128)} %bitcast.1.len_ref, s32[32,4]{1,0:T(8,128)S(1)} %copy.5.paths_ref), custom_call_target="tpu_custom_call" | custom-call | flops 1073741824 | bytes 4194304 | tf_op jit(solution)/shard_map/pallas_call | solution.py:338
  68.7 0.7 copy.8
Async XLA Ops:
  0.0 0.7 copy-start

commit v7 on v4

--- a/solution.py
+++ b/solution.py
@@ -42,8 +42,8 @@
 
 
 def kernel(
-    q_ref, kv_ref, len_ref, paths_ref, out_ref,
-    qx, qf, qn, qplane, kvz, len_v, paths_v, metav, metas, o_out, o_in, s_out, s_in, ff, fx,
+    q_ref, kv_ref, len_s, paths_s, out_ref,
+    qx, qf, qn, qplane, kvz, metav, metas, o_out, o_in, s_out, s_in, ff, fx,
     x_send, x_recv, kv_send, kv_recv, q_send, q_recv, m_send, m_recv,
     o_send, o_recv, s_send, s_recv, r_send, r_recv, own_sem,
 ):
@@ -68,12 +68,9 @@
 
     kv_own = [pltpu.make_async_copy(kv_ref.at[part, 0], kvz.at[0, pl.ds(HEAD + part * TOKENS, TOKENS)],
                                     own_sem.at[part]) for part in (0, 1)]
-    small = [pltpu.make_async_copy(len_ref, len_v, own_sem.at[2]),
-             pltpu.make_async_copy(paths_ref, paths_v, own_sem.at[3])]
-    for copy in kv_own + small:
+    for copy in kv_own:
         copy.start()
-    small[0].wait()
-    length = jnp.broadcast_to(len_v[...], (HEAD, DIM))
+    length = jnp.full((HEAD, DIM), len_s[0], jnp.int32)
     upper = lax.broadcasted_iota(jnp.int32, (HEAD, DIM), 0) < HEAD // 2
     kvz[0, 0:HEAD, :] = jnp.where(upper, length >> 8, length & 255).astype(jnp.float32).astype(jnp.bfloat16)
     for copy in kv_own:
@@ -112,14 +109,17 @@
                 kv_copy(side, chunk, hop).wait_send()
                 kv_copy(side, chunk, hop + 1).start()
 
-    small[1].wait()
     row = lax.broadcasted_iota(jnp.int32, (ROWS, DIM), 0)
     col = lax.broadcasted_iota(jnp.int32, (ROWS, DIM), 1)
 
     def upright(line):
         return jnp.sum(jnp.where(row == col, line, 0), axis=1, keepdims=True)
 
-    level = [paths_v[:, j:j + 1] for j in range(DEPTH)]
+    spread = jnp.zeros((ROWS, DIM), jnp.int32)
+    for r in range(ROWS):
+        for j in range(DEPTH):
+            spread = jnp.where((row == r) & (col == j), paths_s[j, r], spread)
+    level = [spread[:, j:j + 1] for j in range(DEPTH)]
     key = level[0] * ROWS + row[:, 0:1]
     key_line = jnp.sum(jnp.where(row == col, key, 0), axis=0, keepdims=True)
     place_line = jnp.sum(jnp.where(key < key_line, 1, 0), axis=0, keepdims=True)
@@ -329,7 +329,7 @@
     return pl.pallas_call(
         kernel,
         out_shape=jax.ShapeDtypeStruct((rows, width), bf16),
-        in_specs=[anywhere] * 4,
+        in_specs=[anywhere] * 2 + [pl.BlockSpec(memory_space=pltpu.SMEM)] * 2,
         out_specs=anywhere,
         scratch_shapes=[
             pltpu.VMEM((NX, OWN, LANES), bf16),
@@ -337,8 +337,6 @@
             pltpu.VMEM((ROWS, GROUP, DIM), bf16),
             pltpu.VMEM((PLANE, PAIRS, PAIR, DIM), bf16),
             pltpu.VMEM((NZ, HEAD + 2 * TOKENS, DIM), bf16),
-            pltpu.VMEM((1, 1), i32),
-            pltpu.VMEM((ROWS, DEPTH), i32),
             pltpu.VMEM((PLANE, SUB, DIM), i32),
             pltpu.SMEM((PLANE, SUB, DIM), i32),
             pltpu.VMEM((2 * PLANE * NZ, GROUP, DIM), bf16),
@@ -359,7 +357,7 @@
         compiler_params=pltpu.CompilerParams(
             collective_id=0, has_side_effects=True, vmem_limit_bytes=56356864),
         cost_estimate=pl.CostEstimate(flops=1 << 30, bytes_accessed=1 << 22, transcendentals=1 << 21),
-    )(queries, kv_cache, node_len.reshape(1, 1), paths)
+    )(queries, kv_cache, node_len, paths.T)
 
 
 def solution(mesh):

time: 69.6 us -> 70.1 us (level)
  no operation moved by 1% of the time
where the time goes in v7:
time: 70.1 us; the launch traced here: 69.9 us
  Pallas kernels  68.6 us (98%)
    pallas_call x1, Pallas kernels, shards(): pl.pallas_call(kernel, out_shape=jax.ShapeDtypeStruct((rows, width), bf16...  68.6 us

profile of v7, /device:TPU:1, one launch (start us, length us, event | category | flops | bytes accessed | tf_op | source)
XLA Modules:
  0.0 69.9 jit_solution(14621660498909994440)
XLA Ops:
  0.0 0.0 copy-start
  0.7 0.0 copy-done
  0.7 68.6 %shard_map.46 = bf16[8,8192]{1,0:T(8,128)(2,1)S(1)} custom-call(bf16[8,8192]{1,0:T(8,128)(2,1)} %q_ref.1, bf16[2,1,512,128]{3,2,1,0:T(8,128)(2,1)} %kv_ref.1, s32[1]{0:T(128)S(6)} %copy.6.len_s, s32[4,32]{1,0:T(4,128)S(1)} %bitcast.1), custom_call_target="tpu_custom_call" | custom-call | flops 1073741824 | bytes 4194304 | tf_op jit(solution)/shard_map/pallas_call | solution.py:329
  69.3 0.7 copy.7
Async XLA Ops:
  0.0 0.7 copy-start
